TPU v7x, 32 devices: a whole 2x2x4 slice. The times are simulated.
32 devices in a mesh: section: 4 (over z), dp: 8 (over y, x, core).
Axes of the slice: x: 2, y: 2, z: 4, core: 2. Of those that a mesh axis runs over, the one named last changes fastest.
Arguments:
- query_states: bfloat16 [4, 3584, 2048], P('section', 'dp'), may hold values from -400 to 400
- cache_emb: bfloat16 [32, 128, 896], P('dp'), may hold values from -6 to 6
- nb_owner: int32 [4, 56, 2], P('section', 'dp'), may hold values from 0 to 7, all different within a row; in each aligned block of 7 rows (0 to 6, 7 to 13, ..., all dimensions but the last counted through in order) at most 2 rows name the same one
- nb_row: int32 [4, 56, 2], P('section', 'dp'), may hold values from 0 to 3
- enc_gain: float32 [4, 896], P('section'), may hold values from 0.1 to 1.9
- w_qkv: bfloat16 [4, 896, 2688], P('section'), may hold values from -0.1875 to 0.1875
- w_out: bfloat16 [4, 896, 896], P('section'), may hold values from -0.1875 to 0.1875
- w_kv: bfloat16 [4, 896, 4096], P('section'), may hold values from -0.1875 to 0.1875
Outputs:
- cross_out: bfloat16 [4, 3584, 2048], P('section', 'dp')
Inputs may be any that keep to these rules, and one draw needn't show every extreme that they name: `nb_owner`: the 2 neighbours of one span name different shards; among the spans of one device no shard is named more than 2 times.
All inputs are finite; a program needn't handle non-finite values.
Results may differ from a plain program's by a relative error of at most 0.019.
Values may be sent and summed in bfloat16 or wider, within the bound.
No kernel may reach another device: no remote copies, remote signals or barrier semaphores. Data moves between devices by JAX's collectives and lax.ppermute only.
A program may use at most 128 MiB of HBM per device.

v0:
```python
import math

import jax
import jax.numpy as jnp
from jax import lax
from jax.sharding import PartitionSpec as P

HD = 128
ENC_HD = 64
SPAN = 64
CAP = 2


def shifted(block, axis, distance):
    devices = range(lax.axis_size(axis))
    route = [((i - distance) % len(devices), i) for i in devices]
    return lax.ppermute(block, axis, route)


def encode(tokens, norm_gain, w_qkv, w_out):
    neighbours, length, features = tokens.shape
    head_count = features // ENC_HD
    floats = tokens.astype(jnp.float32)
    factor = lax.rsqrt(jnp.mean(floats * floats, axis=-1, keepdims=True) + 1e-06)
    normed = (floats * factor * norm_gain).astype(jnp.bfloat16)
    projected = jnp.einsum("mte,ef->mtf", normed, w_qkv, preferred_element_type=jnp.float32).astype(
        jnp.bfloat16
    )
    enc_queries = projected[..., :features].reshape(neighbours, length, head_count, ENC_HD)
    enc_keys = projected[..., features : 2 * features].reshape(
        neighbours, length, head_count, ENC_HD
    )
    enc_values = projected[..., 2 * features :].reshape(neighbours, length, head_count, ENC_HD)
    scores = jnp.einsum(
        "mqhd,mkhd->mhqk", enc_queries, enc_keys, preferred_element_type=jnp.float32
    ) / math.sqrt(ENC_HD)
    powers = jnp.exp(scores)
    weights = (powers / jnp.sum(powers, axis=-1, keepdims=True)).astype(jnp.bfloat16)
    context = jnp.einsum(
        "mhqk,mkhd->mqhd", weights, enc_values, preferred_element_type=jnp.float32
    ).astype(jnp.bfloat16)
    context = context.reshape(neighbours, length, features)
    branch = jnp.einsum("mte,ef->mtf", context, w_out, preferred_element_type=jnp.float32)
    return (floats + branch).astype(jnp.bfloat16)


def cross_attend(encoded, queries, w_kv):
    keyvals = jnp.einsum("mte,ef->mtf", encoded, w_kv, preferred_element_type=jnp.float32).astype(
        jnp.bfloat16
    )
    half_width = w_kv.shape[1] // 2
    head_count = half_width // HD
    spans = queries.shape[0] // SPAN
    cross_keys = keyvals[..., :half_width].reshape(spans, -1, head_count, HD)
    cross_values = keyvals[..., half_width:].reshape(spans, -1, head_count, HD)
    grouped = queries.reshape(spans, SPAN, head_count, HD)
    scores = jnp.einsum(
        "cqhd,ckhd->chqk", grouped, cross_keys, preferred_element_type=jnp.float32
    ) / math.sqrt(HD)
    highest = jnp.max(scores, axis=-1, keepdims=True)
    powers = jnp.exp(scores - highest)
    weights = (powers / jnp.sum(powers, axis=-1, keepdims=True)).astype(jnp.bfloat16)
    output = jnp.einsum(
        "chqk,ckhd->cqhd", weights, cross_values, preferred_element_type=jnp.float32
    ).astype(jnp.bfloat16)
    return output.reshape(spans * SPAN, half_width)


def shards(query_states, cache_emb, nb_owner, nb_row, enc_gain, w_qkv, w_out, w_kv):
    received = shifted(query_states, "section", 1)
    owners = nb_owner[0].reshape(-1)
    rows_local = nb_row[0].reshape(-1)
    row_length = cache_emb.shape[1]
    features = cache_emb.shape[2]
    dp_count = lax.axis_size("dp")
    owner_hits = (owners[:, None] == jnp.arange(dp_count, dtype=jnp.int32)[None, :]).astype(
        jnp.int32
    )
    earlier = jnp.cumsum(owner_hits, axis=0) - owner_hits
    slot_index = jnp.sum(earlier * owner_hits, axis=1)
    slot_hits = (slot_index[:, None] == jnp.arange(CAP, dtype=jnp.int32)[None, :]).astype(jnp.int32)
    marked = owner_hits[:, :, None] * slot_hits[:, None, :] * (rows_local + 1)[:, None, None]
    requests = jnp.sum(marked, axis=0) - 1
    served = lax.all_to_all(requests, "dp", split_axis=0, concat_axis=0, tiled=True)
    picked = jnp.take(cache_emb, jnp.maximum(served, 0).reshape(-1), axis=0)
    picked = picked.reshape(dp_count, CAP, row_length, features)
    returned = lax.all_to_all(picked, "dp", split_axis=0, concat_axis=0, tiled=True)
    flattened = returned.reshape(dp_count * CAP, row_length, features)
    tokens = jnp.take(flattened, owners * CAP + slot_index, axis=0)
    encoded = encode(tokens, enc_gain[0], w_qkv[0], w_out[0])
    result = cross_attend(encoded, received[0], w_kv[0])
    return result[None]


def solution(mesh):
    placed = (
        P("section", "dp", None),
        P("dp", None, None),
        P("section", "dp", None),
        P("section", "dp", None),
        P("section", None),
        P("section", None, None),
        P("section", None, None),
        P("section", None, None),
    )
    return jax.shard_map(
        shards, mesh=mesh, in_specs=placed, out_specs=P("section", "dp", None), check_vma=False
    )
```

profile of v0, /device:TPU:0, one launch (start us, length us, event | category | flops | bytes accessed | tf_op | source)
XLA Modules:
  0.0 216.8 jit_solution(8230973048343278693)
XLA Ops:
  0.0 0.0 copy-start
  0.0 0.9 copy.48
  0.9 0.1 reshape_squeeze.7
  1.0 0.2 reduce_window_sum.11
  1.2 0.7 broadcast_add_fusion
  1.9 0.1 copy.49
  2.0 0.1 add.70
  2.0 0.1 multiply_reduce_fusion
  2.2 0.1 copy.50
  2.3 9.6 %all_to_all.11 = s32[8,1,2]{2,1,0:T(1,128)S(1)} all-to-all(s32[8,1,2]{2,1,0:T(1,128)S(1)} %copy.50), channel_id=1, replica_groups=mesh['section'=4,'dp'=8] {'dp'}, dimensions={0} | all-to-all | bytes 128 | tf_op jit(solution)/shard_map/all_to_all | solution.py:84
  11.9 0.1 reshape.166
  12.0 0.1 copy.51
  12.1 0.1 copy.52
  12.2 3.9 %gather_fusion = bf16[16,128,896]{2,1,0:T(8,128)(2,1)} fusion(bf16[4,128,896]{2,1,0:T(8,128)(2,1)} %param.9, s32[1024]{0:T(1024)S(1)} %pad_clamp_fusion.1), kind=kCustom, calls=%fused_computation | custom fusion | bytes 7340096 | tf_op jit(solution)/shard_map/jit(_take)/gather | solution.py:85
  16.2 4.3 %broadcast_select_fusion = bf16[8,2,128,896]{3,2,1,0:T(8,128)(2,1)} fusion(bf16[8,2,128,896]{3,2,1,0:T(8,128)(2,1)} %bitcast.72, pred[8,2]{1,0:T(8,128)(4,1)S(1)} %copy.52), kind=kLoop, calls=%fused_computation.30 | loop fusion | flops 1835008 | bytes 7340048 | tf_op jit(solution)/shard_map/jit(_take)/select_n | solution.py:85
  20.5 0.0 copy-start.3
  20.5 0.0 copy-start.4
  20.5 4.6 %all-to-all-start.1 = ((bf16[8,2,128,896]{3,2,1,0:T(8,128)(2,1)}), bf16[8,2,128,896]{3,2,1,0:T(8,128)(2,1)}, u32[]{:S(2)}, u32[]{:S(2)}) async-start(bf16[8,2,128,896]{3,2,1,0:T(8,128)(2,1)} %broadcast_select_fusion), calls=%async_computation.1 | async-start | bytes 7340032 | tf_op jit(solution)/shard_map/all_to_all | solution.py:87
  25.1 1.6 collective-permute-start
  26.7 0.0 copy-done.3
  26.7 0.1 copy.53
  26.8 0.1 mul.70
  26.9 0.0 copy-done.4
  27.0 42.5 %collective-permute-done = bf16[1,448,2048]{2,1,0:T(8,128)(2,1)S(1)} collective-permute-done((bf16[1,448,2048]{2,1,0:T(8,128)(2,1)}, bf16[1,448,2048]{2,1,0:T(8,128)(2,1)S(1)}, u32[]{:S(2)}, u32[]{:S(2)}) %collective-permute-start) | collective-permute-done | bytes 1835040 | tf_op jit(solution)/shard_map/ppermute | solution.py:17
  69.5 0.0 copy-start.2
  69.5 1.2 copy-done.2
  70.7 2.0 copy.66
  72.7 0.0 all-to-all-done.1
  72.7 4.7 %gather_fusion.1 = bf16[14,128,896]{2,1,0:T(8,128)(2,1)} fusion(bf16[16,128,896]{2,1,0:T(8,128)(2,1)} %bitcast.3, s32[1024]{0:T(1024)S(1)} %pad_clamp_fusion), kind=kCustom, calls=%fused_computation.1 | custom fusion | bytes 6422584 | tf_op jit(solution)/shard_map/jit(_take)/gather | solution.py:89
  77.5 2.9 %fusion.10 = f32[14,128]{1,0:T(8,128)S(1)} fusion(bf16[14,128,896]{2,1,0:T(8,128)(2,1)} %gather_fusion.1, pred[14]{0:T(512)(128)(4,1)S(1)} %compare_and_fusion), kind=kLoop, calls=%fused_computation.22 | loop fusion | flops 6420736 | bytes 3218446 | tf_op jit(solution)/shard_map/reduce_sum | solution.py:24
  80.4 14.6 %convolution_convert_fusion.1 = bf16[14,128,2688]{2,1,0:T(8,128)(2,1)S(1)} fusion(bf16[1,896,2688]{2,1,0:T(8,128)(2,1)} %param.13, f32[896]{0:T(1024)S(1)} %reduce.1, f32[14,128]{1,0:T(8,128)S(1)} %add_rsqrt_fusion, bf16[14,128,896]{2,1,0:T(8,128)(2,1)} %gather_fusion.1, pred[14]{0:T(512)(128)(4,1)S(1)} %compare_and_fusion), kind=kOutput, calls=%fused_computation.10 | convolution fusion | flops 8644722688 | bytes 17672718 | tf_op jit(solution)/shard_map/mte,ef->mtf/dot_general | solution.py:26
  95.0 3.8 %fusion.44 = (bf16[14,128,896]{2,1,0:T(8,128)(2,1)}, bf16[14,128,896]{2,1,0:T(8,128)(2,1)}, bf16[14,128,896]{2,1,0:T(8,128)(2,1)}) fusion(bf16[14,128,2688]{2,1,0:T(8,128)(2,1)S(1)} %convolution_convert_fusion.1), kind=kLoop, calls=%fused_computation.62 | loop fusion | bytes 19267584 | tf_op jit(solution)/shard_map/slice | solution.py:30
  98.8 5.6 %copy.56 = bf16[14,128,896]{1,2,0:T(8,128)(2,1)} copy(bf16[14,128,896]{2,1,0:T(8,128)(2,1)} %get-tuple-element.7) | data formatting | bytes 6422528 | tf_op jit(solution)/shard_map/slice | solution.py:30
  104.4 5.6 %copy.55 = bf16[14,128,896]{1,2,0:T(8,128)(2,1)} copy(bf16[14,128,896]{2,1,0:T(8,128)(2,1)} %get-tuple-element.8) | data formatting | bytes 6422528 | tf_op jit(solution)/shard_map/slice | solution.py:29
  110.0 5.6 %copy.54 = bf16[14,128,896]{1,2,0:T(8,128)(2,1)} copy(bf16[14,128,896]{2,1,0:T(8,128)(2,1)} %get-tuple-element.9) | data formatting | bytes 6422528 | tf_op jit(solution)/shard_map/slice | solution.py:33
  115.6 5.7 %fusion.1 = (f32[14,14,128]{2,1,0:T(8,128)S(1)}, f32[14,14,128,128]{2,3,1,0:T(8,128)S(1)}) fusion(bf16[14,128,14,64]{1,3,2,0:T(8,128)(2,1)} %bitcast.74, bf16[14,128,14,64]{1,3,2,0:T(8,128)(2,1)} %bitcast.73), kind=kOutput, calls=%fused_computation.5 | convolution fusion | flops 417439232 | bytes 19367936 | tf_op jit(solution)/shard_map/mqhd,mkhd->mhqk/dot_general | solution.py:34
  121.3 5.7 %fusion.26 = bf16[14,14,64,128]{3,2,1,0:T(8,128)(2,1)} fusion(bf16[14,128,14,64]{1,3,2,0:T(8,128)(2,1)} %bitcast.77, f32[14,14,128,128]{2,3,1,0:T(8,128)S(1)} %get-tuple-element.11, f32[14,14,128]{2,1,0:T(8,128)S(1)} %get-tuple-element.10), kind=kOutput, calls=%fused_computation.35 | convolution fusion | flops 422281216 | bytes 19367936 | tf_op jit(solution)/shard_map/mhqk,mkhd->mqhd/dot_general | solution.py:39
  127.1 0.0 copy-done
  127.1 26.6 %convolution_convert_fusion = bf16[14,128,4096]{2,1,0:T(8,128)(2,1)} fusion(bf16[1,896,4096]{2,1,0:T(8,128)(2,1)} %param.15, bf16[14,128,896]{1,2,0:T(8,128)(2,1)} %bitcast.80, bf16[1,896,896]{2,1,0:T(8,128)(2,1)S(1)} %copy-done, bf16[14,128,896]{2,1,0:T(8,128)(2,1)} %gather_fusion.1, pred[14]{0:T(512)(128)(4,1)S(1)} %compare_and_fusion), kind=kOutput, calls=%fused_computation.6 | convolution fusion | flops 16044392448 | bytes 30048270 | tf_op jit(solution)/shard_map/mte,ef->mtf/dot_general | solution.py:48
  153.6 9.0 %fusion.43 = (bf16[14,128,2048]{2,1,0:T(8,128)(2,1)}, bf16[14,128,2048]{2,1,0:T(8,128)(2,1)S(1)}) fusion(bf16[14,128,4096]{2,1,0:T(8,128)(2,1)} %convolution_convert_fusion), kind=kLoop, calls=%fused_computation.61 | loop fusion | bytes 29360128 | tf_op jit(solution)/shard_map/slice | solution.py:54
  162.7 8.8 %copy.65 = bf16[224,8,16,128]{3,2,1,0:T(8,128)(2,1)} copy(bf16[224,8,16,128]{3,1,2,0:T(8,128)(2,1)} %bitcast.70) | data formatting | bytes 14680064
  171.5 8.8 %fusion.7 = f32[7,16,256,64]{2,3,1,0:T(8,128)} fusion(bf16[7,256,16,128]{3,2,1,0:T(8,128)(2,1)} %bitcast.71, bf16[7,64,16,128]{3,2,1,0:T(8,128)(2,1)S(1)} %bitcast.76), kind=kOutput, calls=%fused_computation.18 | convolution fusion | flops 469762048 | bytes 16515072 | tf_op jit(solution)/shard_map/cqhd,ckhd->chqk/dot_general | solution.py:57
  180.2 7.9 %fusion.45 = f32[7,16,64]{2,1,0:T(8,128)S(1)} fusion(f32[7,16,256,64]{2,3,1,0:T(8,128)} %fusion.7), kind=kOutput, calls=%fused_computation.63 | output fusion | flops 7340287 | bytes 7368704 | tf_op jit(solution)/shard_map/sub | solution.py:61
  188.2 5.7 %copy.67 = bf16[224,8,16,128]{3,2,1,0:T(8,128)(2,1)} copy(bf16[224,8,16,128]{3,1,2,0:T(8,128)(2,1)S(1)} %bitcast.69) | data formatting | bytes 14680064
  193.9 0.0 copy-start.1
  193.9 18.2 %convert_bitcast_fusion = bf16[7,64,16,128]{3,1,2,0:T(8,128)(2,1)} fusion(bf16[7,256,16,128]{3,2,1,0:T(8,128)(2,1)} %bitcast.75, f32[7,16,64]{2,1,0:T(8,128)S(1)} %fusion.45, f32[7,16,256,64]{2,3,1,0:T(8,128)} %fusion.7), kind=kOutput, calls=%fused_computation.37 | convolution fusion | flops 479862016 | bytes 16543744 | tf_op jit(solution)/shard_map/chqk,ckhd->cqhd/dot_general | solution.py:63
  212.1 2.7 %copy.62 = bf16[7,64,16,128]{3,2,1,0:T(8,128)(2,1)S(1)} copy(bf16[7,64,16,128]{3,1,2,0:T(8,128)(2,1)} %convert_bitcast_fusion) | data formatting | bytes 3670016 | tf_op jit(solution)/shard_map/convert_element_type | solution.py:65
  214.8 1.7 broadcast_in_dim_reshape.3
  216.6 0.0 copy-done.1
  (13 shorter events, 0.1 us)
Async XLA Ops:
  0.0 127.1 %copy-start = (bf16[1,896,896]{2,1,0:T(8,128)(2,1)S(1)}, bf16[1,896,896]{2,1,0:T(8,128)(2,1)}, u32[]{:S(2)}) copy-start(bf16[1,896,896]{2,1,0:T(8,128)(2,1)} %param.14) | copy-start | bytes 4816900
  20.5 6.3 %copy-start.3 = (s32[1,7,2]{1,2,0:T(2,128)S(1)}, s32[1,7,2]{1,2,0:T(2,128)}, u32[]{:S(2)}) copy-start(s32[1,7,2]{1,2,0:T(2,128)} %param.10) | copy-start | bytes 172
  20.5 6.5 %copy-start.4 = (f32[1,896]{1,0:T(1,128)S(1)}, f32[1,896]{1,0:T(1,128)}, u32[]{:S(2)}) copy-start(f32[1,896]{1,0:T(1,128)} %param.12) | copy-start | bytes 10756
  20.5 52.2 %all-to-all-start.1 = ((bf16[8,2,128,896]{3,2,1,0:T(8,128)(2,1)}), bf16[8,2,128,896]{3,2,1,0:T(8,128)(2,1)}, u32[]{:S(2)}, u32[]{:S(2)}) async-start(bf16[8,2,128,896]{3,2,1,0:T(8,128)(2,1)} %broadcast_select_fusion), calls=%async_computation.1 | async-start | bytes 7340032 | tf_op jit(solution)/shard_map/all_to_all | solution.py:87
  25.1 44.4 %collective-permute-start = (bf16[1,448,2048]{2,1,0:T(8,128)(2,1)}, bf16[1,448,2048]{2,1,0:T(8,128)(2,1)S(1)}, u32[]{:S(2)}, u32[]{:S(2)}) collective-permute-start(bf16[1,448,2048]{2,1,0:T(8,128)(2,1)} %param.8), channel_id=1, source_target_pairs={{24,0},{0,8},{8,16},{16,24},{25,1},{1,9},{9,17},{17,25},{26,2},{2,... | collective-permute-start | bytes 5505032 | tf_op jit(solution)/shard_map/ppermute | solution.py:17
  69.5 1.2 copy-start.2
  193.9 22.7 %copy-start.1 = (bf16[1,896,896]{2,1,0:T(8,128)(2,1)S(1)}, bf16[1,896,896]{2,1,0:T(8,128)(2,1)}, u32[]{:S(2)}) copy-start(bf16[1,896,896]{2,1,0:T(8,128)(2,1)} %param.14) | copy-start | bytes 4816900
where the time goes:
time: 221 us; the launch traced here: 217 us
  matrix products  79.6 us (36%)
  local copies, waits for them, and re-layouts  62.2 us (28%)
  waiting for transfers between devices  42.5 us (19%)
  other arithmetic  16.2 us (7%)
  blocking collectives  9.62 us (4%)
  starting transfers between devices  6.26 us (3%)
    ppermute x1, waiting for transfers between devices, shifted(): return lax.ppermute(block, axis, route)  42.5 us
    dot_general x1, matrix products, cross_attend(): jnp.einsum('mte,ef->mtf', encoded, w_kv, preferred_element_type=jnp.float32)  26.6 us
    unnamed x14, local copies, waits for them, and re-layouts  18.7 us
    dot_general x1, matrix products, cross_attend(): jnp.einsum('chqk,ckhd->cqhd', weights, cross_values, preferred_element_ty...  18.2 us
    dot_general x1, matrix products, encode(): jnp.einsum('mte,ef->mtf', normed, w_qkv, preferred_element_type=jnp.float32)  14.6 us
    all_to_all x1, blocking collectives, shards(): lax.all_to_all(requests, 'dp', split_axis=0, concat_axis=0, tiled=True)  9.62 us
    slice x2, local copies, waits for them, and re-layouts, encode(): projected[..., features:2 * features]  9.39 us
    slice x1, local copies, waits for them, and re-layouts, cross_attend(): cross_keys = keyvals[..., :half_width].reshape(spans, -1, head_count, HD)  9.03 us
  transfers between devices with their start and end apart: 2, of which 1 were waited for; matrix products, arithmetic and copies ran while one was open for 1% of the time, Pallas kernels for 0%

commit v1 on v0

v1 whole, which is shorter than its diff:
```python
import functools
import math

import jax
import jax.numpy as jnp
from jax import lax
from jax.experimental import pallas as pl
from jax.experimental.pallas import tpu as pltpu
from jax.sharding import PartitionSpec as P

HD = 128
ENC_HD = 64
SPAN = 64
LOG2E = 1.4426950408889634
BF = jnp.bfloat16
F32 = jnp.float32
MB = 2**20
ANY = pl.BlockSpec(memory_space=pl.ANY)
VM = pl.BlockSpec(memory_space=pltpu.VMEM)
SM = pl.BlockSpec(memory_space=pltpu.SMEM)
EARLY = 5
E_US, KV_US, CROSS_US = 8.0, 4.0, 6.0


def cost(us):
    return pl.CostEstimate(flops=int(us * 1.0e9), bytes_accessed=1, transcendentals=0)


def encode_kernel(
    rows_ref, gain_ref, wqkv_hbm, wout_hbm, out_ref, wqkv, wout, proj, ctx, sems
):
    count, length, width = rows_ref.shape
    step = width // 4
    pieces = [
        [
            pltpu.make_async_copy(
                wqkv_hbm.at[0, pl.ds(j * step, step), pl.ds(i * width, width)],
                wqkv.at[pl.ds(j * step, step), pl.ds(i * width, width)],
                sems.at[4 * i + j],
            )
            for j in range(4)
        ]
        for i in range(3)
    ]
    last = pltpu.make_async_copy(wout_hbm.at[0], wout, sems.at[12])
    for piece in pieces:
        for copy in piece:
            copy.start()
    last.start()
    tokens = rows_ref[...].reshape(count * length, width)
    floats = tokens.astype(F32)
    factor = lax.rsqrt(jnp.mean(floats * floats, axis=-1, keepdims=True) + 1e-06)
    ctx[...] = (floats * factor * gain_ref[...]).astype(BF)
    for i, piece in enumerate(pieces):
        for copy in piece:
            copy.wait()
        cols = slice(i * width, (i + 1) * width)
        proj[:, cols] = jnp.dot(ctx[...], wqkv[:, cols], preferred_element_type=F32).astype(BF)
    lane = lax.broadcasted_iota(jnp.int32, (length, 2 * ENC_HD), 1)
    first = lane < ENC_HD
    zero = jnp.zeros((length, 2 * ENC_HD), BF)
    scale = LOG2E / math.sqrt(ENC_HD)
    column = lax.broadcasted_iota(jnp.int32, (2 * length, 2 * length), 1)
    line = lax.broadcasted_iota(jnp.int32, (2 * length, 2 * length), 0)
    same = jnp.where((column < length) == (line < length), 1.0, 0.0).astype(BF)
    pairs = width // (2 * ENC_HD)
    for r in range(count):
        spot = slice(r * length, (r + 1) * length)

        def split(base):
            both = proj[spot, base : base + 2 * ENC_HD]
            return jnp.concatenate([jnp.where(first, both, zero), jnp.where(first, zero, both)], axis=0)

        scores = []
        for p in range(pairs):
            base = p * 2 * ENC_HD
            q2 = proj[spot, base : base + 2 * ENC_HD]
            scores.append(
                lax.dot_general(q2, split(width + base), (((1,), (1,)), ((), ())), preferred_element_type=F32)
            )
        powers = [jnp.exp2(part * scale) for part in scores]
        sums = [jnp.dot(part.astype(BF), same, preferred_element_type=F32) for part in powers]
        weights = [(part * (1.0 / total)).astype(BF) for part, total in zip(powers, sums)]
        for p in range(pairs):
            base = p * 2 * ENC_HD
            out = jnp.dot(weights[p], split(2 * width + base), preferred_element_type=F32)
            ctx[spot, base : base + 2 * ENC_HD] = out.astype(BF)
    last.wait()
    branch = jnp.dot(ctx[...], wout[...], preferred_element_type=F32)
    floats = rows_ref[...].reshape(count * length, width).astype(F32)
    out_ref[...] = (floats + branch).astype(BF).reshape(count, length, width)


def encode(rows, gain, w_qkv, w_out):
    count, length, width = rows.shape
    tokens = count * length
    return pl.pallas_call(
        encode_kernel,
        out_shape=jax.ShapeDtypeStruct(rows.shape, BF),
        in_specs=[VM, VM, ANY, ANY],
        out_specs=VM,
        scratch_shapes=[
            pltpu.VMEM((width, 3 * width), BF),
            pltpu.VMEM((width, width), BF),
            pltpu.VMEM((tokens, 3 * width), BF),
            pltpu.VMEM((tokens, width), BF),
            pltpu.SemaphoreType.DMA((13,)),
        ],
        compiler_params=pltpu.CompilerParams(vmem_limit_bytes=52 * MB),
        cost_estimate=cost(E_US),
        name="encode_rows",
    )(rows, gain, w_qkv, w_out)


def gather_rows(plan, sources, owner_ref, row_ref, me, rows, slots, sems, taken):
    spans, picks = owner_ref.shape[1:]

    def look(s, found):
        owner = owner_ref[0, s // picks, lax.rem(s, picks)]
        row = row_ref[0, s // picks, lax.rem(s, picks)]
        if taken is not None:
            taken[s] = 0
        for source, test, place in plan(sources, owner, jnp.bitwise_xor(owner, me), row):

            @pl.when(test)
            def _():
                slots[found] = s
                if taken is not None:
                    taken[s] = 1
                pltpu.make_async_copy(source.at[place], rows.at[found], sems.at[found]).start()

            found = found + test.astype(jnp.int32)
        return found

    return lax.fori_loop(0, spans * picks, look, jnp.int32(0))


def project_pairs(found, source, w_ref, rows, sems, finish, after):
    length, width = rows.shape[1:]
    chunk = 1024

    def project(g, carry):
        i = 2 * g
        pltpu.make_async_copy(source.at[0], rows.at[i], sems.at[i]).wait()

        @pl.when(i + 1 < found)
        def _():
            pltpu.make_async_copy(source.at[0], rows.at[i + 1], sems.at[i + 1]).wait()

        both = rows[pl.ds(i, 2)].reshape(2 * length, width)
        for b in range(w_ref.shape[1] // chunk):
            cols = pl.ds(b * chunk, chunk)
            out = jnp.dot(both, w_ref[:, cols], preferred_element_type=F32).astype(BF)
            finish(i, cols, out[:length], out[length:])
        after(i)
        return carry

    lax.fori_loop(0, (found + 1) // 2, project, 0)


def kv_kernel(plan, n_src, fresh, *refs):
    owner_ref, row_ref, me_ref, w_in = refs[:4]
    sources = refs[4 : 4 + n_src]
    kv_hbm, w_ref, token_ref, rows, made, slots, sems, w_sem, out_sems = refs[-9:]
    if fresh:
        step = w_ref.shape[0] // 8
        loads = [
            pltpu.make_async_copy(w_in.at[0, pl.ds(i * step, step)], w_ref.at[pl.ds(i * step, step)], w_sem.at[i])
            for i in range(8)
        ]
        for load in loads:
            load.start()
    found = gather_rows(plan, sources, owner_ref, row_ref, me_ref[0], rows, slots, sems, None)
    if fresh:
        for load in loads:
            load.wait()

    def store(i):
        return pltpu.make_async_copy(made.at[i], kv_hbm.at[slots[i]], out_sems.at[i])

    def finish(i, cols, one, two):
        made[i, :, cols] = one
        made[i + 1, :, cols] = two

    def send(i):
        store(i).start()

        @pl.when(i + 1 < found)
        def _():
            store(i + 1).start()

    def drain(i, carry):
        store(i).wait()
        return carry

    project_pairs(found, sources[0], w_ref, rows, sems, finish, send)
    lax.fori_loop(0, found, drain, 0)
    token_ref[...] = jnp.zeros_like(token_ref)


def keyvals_part(owner, row, me, sources, w_kv, before, plan, most):
    length, width = sources[0].shape[1:]
    features = w_kv.shape[-1]
    slots = owner.shape[1] * owner.shape[2]
    most = min(most, slots)
    most += most % 2
    fresh = before is None
    operands = [owner, row, me, w_kv, *sources]
    specs = [SM, SM, SM, ANY if fresh else VM] + [ANY] * len(sources)
    aliases = {}
    if not fresh:
        aliases = {3: 1, len(operands): 0}
        operands.append(before)
        specs.append(ANY)
    return pl.pallas_call(
        functools.partial(kv_kernel, plan, len(sources), fresh),
        out_shape=[
            jax.ShapeDtypeStruct((slots, length, features), BF),
            pltpu.VMEM((width, features), BF),
            jax.ShapeDtypeStruct((8, 128), F32),
        ],
        in_specs=specs,
        out_specs=[ANY, VM, VM],
        input_output_aliases=aliases,
        scratch_shapes=[
            pltpu.VMEM((most, length, width), BF),
            pltpu.VMEM((most, length, features), BF),
            pltpu.SMEM((most,), jnp.int32),
            pltpu.SemaphoreType.DMA((most,)),
            pltpu.SemaphoreType.DMA((8,)),
            pltpu.SemaphoreType.DMA((most,)),
        ],
        compiler_params=pltpu.CompilerParams(vmem_limit_bytes=48 * MB),
        cost_estimate=cost(KV_US),
        name="keyvals_rows",
    )(*operands)


def attend_span(span, queries, kv_ref, out_ref):
    width = queries.shape[1]
    picks, length = 2, kv_ref.shape[1]
    keys = picks * length
    lane = lax.broadcasted_iota(jnp.int32, (SPAN, 2 * HD), 1)
    first = lane < HD
    zero = jnp.zeros((SPAN, 2 * HD), BF)
    scale = LOG2E / math.sqrt(HD)
    pairs = width // (2 * HD)
    here = pl.ds(pl.multiple_of(span * SPAN, SPAN), SPAN)
    scores = []
    for h in range(pairs):
        cols = slice(h * 2 * HD, (h + 1) * 2 * HD)
        q = queries[here, cols]
        qq = jnp.concatenate([jnp.where(first, q, zero), jnp.where(first, zero, q)], axis=0)
        k = kv_ref[pl.ds(span * picks, picks), :, cols].reshape(keys, 2 * HD)
        scores.append(lax.dot_general(qq, k, (((1,), (1,)), ((), ())), preferred_element_type=F32))
    weights = []
    for part in scores:
        highest = jnp.max(part, axis=-1, keepdims=True)
        powers = jnp.exp2((part - highest) * scale)
        weights.append((powers.astype(BF), 1.0 / jnp.sum(powers, axis=-1, keepdims=True)))
    for h in range(pairs):
        cols = slice(h * 2 * HD, (h + 1) * 2 * HD)
        values = slice(width + h * 2 * HD, width + (h + 1) * 2 * HD)
        v = kv_ref[pl.ds(span * picks, picks), :, values].reshape(keys, 2 * HD)
        both = jnp.dot(weights[h][0], v, preferred_element_type=F32) * weights[h][1]
        out_ref[here, cols] = jnp.where(first, both[:SPAN], both[SPAN:]).astype(BF)


def final_kernel(plan, n_src, *refs):
    owner_ref, row_ref, me_ref, w_ref, kv_hbm, first_hbm, second_hbm = refs[:7]
    sources = refs[7 : 7 + n_src]
    out_hbm, rows, keyvals, queries, result, slots, taken, sems, kv_sems, q_sems, out_sems = refs[7 + n_src :]
    cut = first_hbm.shape[1]
    tokens = queries.shape[0]
    picks = owner_ref.shape[2]
    total = owner_ref.shape[1] * picks
    found = gather_rows(plan, sources, owner_ref, row_ref, me_ref[0], rows, slots, sems, taken)
    loads = [
        pltpu.make_async_copy(first_hbm.at[0], queries.at[pl.ds(0, cut)], q_sems.at[0]),
        pltpu.make_async_copy(second_hbm.at[0], queries.at[pl.ds(cut, tokens - cut)], q_sems.at[1]),
    ]
    for load in loads:
        load.start()

    def fetch(s):
        return pltpu.make_async_copy(kv_hbm.at[s], keyvals.at[s], kv_sems.at[s])

    def begin(s, carry):
        @pl.when(taken[s] == 0)
        def _():
            fetch(s).start()

        return carry

    lax.fori_loop(0, total, begin, 0)

    def finish(i, cols, one, two):
        keyvals[slots[i], :, cols] = one

        @pl.when(i + 1 < found)
        def _():
            keyvals[slots[i + 1], :, cols] = two

    if n_src:
        project_pairs(found, sources[0], w_ref, rows, sems, finish, lambda i: None)
    for load in loads:
        load.wait()

    def store(span):
        here = pl.ds(pl.multiple_of(span * SPAN, SPAN), SPAN)
        return pltpu.make_async_copy(result.at[here], out_hbm.at[0, here], out_sems.at[span])

    def attend(span, carry):
        for j in range(picks):
            s = span * picks + j

            @pl.when(taken[s] == 0)
            def _():
                fetch(s).wait()

        attend_span(span, queries, keyvals, result)
        store(span).start()
        return carry

    lax.fori_loop(0, tokens // SPAN, attend, 0)

    def drain(span, carry):
        store(span).wait()
        return carry

    lax.fori_loop(0, tokens // SPAN, drain, 0)


def final(owner, row, me, sources, w, kv, first, second, plan, most):
    length, width = kv.shape[1], w.shape[0]
    slots = owner.shape[1] * owner.shape[2]
    tokens, features = first.shape[1] + second.shape[1], first.shape[2]
    return pl.pallas_call(
        functools.partial(final_kernel, plan, len(sources)),
        out_shape=jax.ShapeDtypeStruct((1, tokens, features), BF),
        in_specs=[SM, SM, SM, VM] + [ANY] * (3 + len(sources)),
        out_specs=ANY,
        scratch_shapes=[
            pltpu.VMEM((most, length, width), BF),
            pltpu.VMEM((slots, length, kv.shape[2]), BF),
            pltpu.VMEM((tokens, features), BF),
            pltpu.VMEM((tokens, features), BF),
            pltpu.SMEM((most,), jnp.int32),
            pltpu.SMEM((slots,), jnp.int32),
            pltpu.SemaphoreType.DMA((most,)),
            pltpu.SemaphoreType.DMA((slots,)),
            pltpu.SemaphoreType.DMA((2,)),
            pltpu.SemaphoreType.DMA((tokens // SPAN,)),
        ],
        compiler_params=pltpu.CompilerParams(vmem_limit_bytes=36 * MB),
        cost_estimate=cost(CROSS_US),
        name="attend_spans",
    )(owner, row, me, w, kv, first, second, *sources)


def head_kernel(q_ref, out_ref, sem):
    copy = pltpu.make_async_copy(q_ref.at[:, pl.ds(0, out_ref.shape[1])], out_ref, sem)
    copy.start()
    copy.wait()


def head(queries, count):
    return pl.pallas_call(
        head_kernel,
        out_shape=pltpu.VMEM((1, count, queries.shape[2]), BF),
        in_specs=[ANY],
        out_specs=VM,
        scratch_shapes=[pltpu.SemaphoreType.DMA],
        compiler_params=pltpu.CompilerParams(vmem_limit_bytes=56 * MB),
        cost_estimate=cost(1.0),
        name="first_queries",
    )(queries)


def split_kernel(start, x_ref, y_ref, q_ref, done_ref, token_ref, low_ref, high_ref, out_ref, x_out, y_out, sems):
    half = low_ref.shape[0]
    copies = [
        pltpu.make_async_copy(x_ref.at[pl.ds(0, half)], low_ref, sems.at[0]),
        pltpu.make_async_copy(y_ref.at[pl.ds(half, high_ref.shape[0])], high_ref, sems.at[1]),
        pltpu.make_async_copy(q_ref.at[:, pl.ds(start, out_ref.shape[1])], out_ref, sems.at[2]),
    ]
    for copy in copies:
        copy.start()
    for copy in copies:
        copy.wait()


def split(x, y, queries, start, received, token):
    _, tokens, width = queries.shape
    half = x.shape[0] // 2
    return pl.pallas_call(
        functools.partial(split_kernel, start),
        out_shape=[
            pltpu.VMEM((half,) + x.shape[1:], BF),
            pltpu.VMEM((y.shape[0] - half,) + x.shape[1:], BF),
            pltpu.VMEM((1, tokens - start, width), BF),
            jax.ShapeDtypeStruct(x.shape, BF),
            jax.ShapeDtypeStruct(y.shape, BF),
        ],
        in_specs=[ANY, ANY, ANY, ANY, VM],
        out_specs=[VM] * 3 + [ANY] * 2,
        input_output_aliases={0: 3, 1: 4},
        scratch_shapes=[pltpu.SemaphoreType.DMA((3,))],
        compiler_params=pltpu.CompilerParams(vmem_limit_bytes=24 * MB),
        cost_estimate=cost(1.0),
        name="next_sends",
    )(x, y, queries, received, token)


def relay_kernel(low_ref, high_ref, token_ref, low_out, high_out):
    pass


def relay(low, high, token):
    return pl.pallas_call(
        relay_kernel,
        out_shape=[jax.ShapeDtypeStruct(low.shape, BF), jax.ShapeDtypeStruct(high.shape, BF)],
        in_specs=[ANY, ANY, ANY],
        out_specs=[ANY, ANY],
        input_output_aliases={0: 0, 1: 1},
        cost_estimate=cost(0.1),
        name="after_rows",
    )(low, high, token)


def shifted(block):
    n = lax.axis_size("section")
    return lax.ppermute(block, "section", [((i - 1) % n, i) for i in range(n)])


def swapped(block, hop):
    n = lax.axis_size("dp")
    return lax.ppermute(block, "dp", [(i, i ^ hop) for i in range(n)])


def shards(query_states, cache_emb, nb_owner, nb_row, enc_gain, w_qkv, w_out, w_kv):
    dp = lax.axis_size("dp")
    slots = nb_owner.shape[1] * nb_owner.shape[2]
    per = cache_emb.shape[0]
    spans = nb_owner.shape[1]
    start = EARLY * spans // 7 * SPAN
    first = shifted(head(query_states, start))
    me = lax.axis_index("dp").astype(jnp.int32).reshape(1)
    own = encode(cache_emb, enc_gain, w_qkv, w_out)
    part = functools.partial(keyvals_part, nb_owner, nb_row, me)
    if dp == 8 and per % 2 == 0:
        half = per // 2
        x, y, near = swapped(own, 2), swapped(own, 4), swapped(own, 1)
        kv, w, token = part([own, near], w_kv, None, lambda src, owner, hop, row: [(src[i], hop == i, row) for i in range(2)], 4)
        xl, yh, rest, x, y = split(x, y, query_states, start, first, token)
        dl, dh, second = swapped(xl, 4), swapped(yh, 2), shifted(rest)
        xs, ys = swapped(x, 1), swapped(y, 1)
        kv, w, token = part(
            [x, xs, y, ys], w, kv, lambda src, owner, hop, row: [(src[i], hop == i + 2, row) for i in range(4)], 8
        )

        def last(src, owner, hop, row):
            lows = [(src[i], (hop == i + 6) & (row < half), row) for i in range(2)]
            return lows + [(src[i + 2], (hop == i + 6) & (row >= half), row - half) for i in range(2)]

        dl, dh = relay(dl, dh, token)
        sources = [dl, swapped(dl, 1), dh, swapped(dh, 1)]
    else:
        whole = lax.all_gather(own, "dp", axis=0, tiled=True)
        second = shifted(query_states[:, start:])
        kv, w, _ = part([whole], w_kv, None, lambda src, owner, hop, row: [(src[0], owner >= 0, owner * per + row)], slots)
        sources = []

        def last(src, owner, hop, row):
            return []

    return final(nb_owner, nb_row, me, sources, w, kv, first, second, last, 4)


def solution(mesh):
    placed = (
        P("section", "dp", None),
        P("dp", None, None),
        P("section", "dp", None),
        P("section", "dp", None),
        P("section", None),
        P("section", None, None),
        P("section", None, None),
        P("section", None, None),
    )
    return jax.shard_map(
        shards, mesh=mesh, in_specs=placed, out_specs=P("section", "dp", None), check_vma=False
    )
```

time: 221 us -> 84.3 us (0.38); the launches traced: 217 us -> 83.9 us
  matrix products: 79.6 us -> 0 us
  local copies, waits for them, and re-layouts: 62.2 us -> 11.1 us
  Pallas kernels: 0 us -> 50.8 us
  waiting for transfers between devices: 42.5 us -> 11 us
  other arithmetic: 16.2 us -> 0 us
  blocking collectives: 9.62 us -> 0 us
  starting transfers between devices: 6.26 us -> 10.9 us
    dot_general x6 -> x0, matrix products: 79.6 us -> none  [the longest x1 26.6 us: cross_attend(): jnp.einsum('mte,ef->mtf', encoded, w_kv, preferred_element_type=jnp.float32)]
    pallas_call x0 -> x7, Pallas kernels: none -> 50.8 us  [the longest x2 24.2 us: keyvals_part(): pl.pallas_call(functools.partial(kv_kernel, plan, len(sources), fresh), o...]
    ppermute x1 -> x11, waiting for transfers between devices: 42.5 us -> 11 us  [the longest x9 11 us: swapped(): return lax.ppermute(block, 'dp', [(i, i ^ hop) for i in range(n)])]
    slice x5 -> x0, local copies, waits for them, and re-layouts: 29.6 us -> none  [the longest x2 9.39 us: encode(): projected[..., features:2 * features]]
    all_to_all x1 -> x0, blocking collectives: 9.62 us -> none  [shards(): lax.all_to_all(requests, 'dp', split_axis=0, concat_axis=0, tiled=True)]
    ppermute x1 -> x11, starting transfers between devices: 1.63 us -> 10.9 us  [the longest x9 6.22 us: swapped(): return lax.ppermute(block, 'dp', [(i, i ^ hop) for i in range(n)])]
    gather x2 -> x0, local copies, waits for them, and re-layouts: 8.68 us -> none  [the longest x1 4.74 us: shards(): tokens = jnp.take(flattened, owners * CAP + slot_index, axis=0)]
    sub x2 -> x0, other arithmetic: 7.92 us -> none  [the longest x1 7.92 us: cross_attend(): powers = jnp.exp(scores - highest)]
  transfers between devices with their start and end apart: 2 -> 11, of which waited for: 1 -> 4; matrix products, arithmetic and copies ran while one was open for 1% -> 2% of each run, Pallas kernels for 0% -> 39%
where the time goes in v1:
time: 84.3 us; the launch traced here: 83.9 us
  Pallas kernels  50.8 us (60%)
  local copies, waits for them, and re-layouts  11.1 us (13%)
  waiting for transfers between devices  11 us (13%)
  starting transfers between devices  10.9 us (13%)
    pallas_call x2, Pallas kernels, keyvals_part(): pl.pallas_call(functools.partial(kv_kernel, plan, len(sources), fresh), o...  24.2 us
    pallas_call x1, Pallas kernels, final(): pl.pallas_call(functools.partial(final_kernel, plan, len(sources)), out_s...  13.9 us
    unnamed x30, local copies, waits for them, and re-layouts  11.1 us
    ppermute x9, waiting for transfers between devices, swapped(): return lax.ppermute(block, 'dp', [(i, i ^ hop) for i in range(n)])  11 us
    pallas_call x1, Pallas kernels, encode(): pl.pallas_call(encode_kernel, out_shape=jax.ShapeDtypeStruct(rows.shape,...  8.91 us
    ppermute x9, starting transfers between devices, swapped(): return lax.ppermute(block, 'dp', [(i, i ^ hop) for i in range(n)])  6.22 us
    ppermute x2, starting transfers between devices, shifted(): return lax.ppermute(block, 'section', [((i - 1) % n, i) for i in range(n)])  4.65 us
    pallas_call x1, Pallas kernels, head(): pl.pallas_call(head_kernel, out_shape=pltpu.VMEM((1, count, queries.shape...  2.38 us
  transfers between devices with their start and end apart: 11, of which 4 were waited for; matrix products, arithmetic and copies ran while one was open for 2% of the time, Pallas kernels for 39%

profile of v1, /device:TPU:0, one launch (start us, length us, event | category | flops | bytes accessed | tf_op | source)
XLA Modules:
  0.0 83.9 jit_solution(3961595267209592161)
XLA Ops:
  0.0 2.4 %first_queries.1 = bf16[1,320,2048]{2,1,0:T(8,128)(2,1)} custom-call(bf16[1,448,2048]{2,1,0:T(8,128)(2,1)} %q_ref.3), custom_call_target="tpu_custom_call" | custom-call | flops 1000000000 | bytes 1 | tf_op jit(solution)/shard_map/first_queries/pallas_call | solution.py:368
  2.4 3.1 %collective-permute-start.3 = (bf16[1,320,2048]{2,1,0:T(8,128)(2,1)}, bf16[1,320,2048]{2,1,0:T(8,128)(2,1)S(1)}, u32[]{:S(2)}, u32[]{:S(2)}) collective-permute-start(bf16[1,320,2048]{2,1,0:T(8,128)(2,1)} %first_queries.1), channel_id=1, source_target_pairs={{24,0},{0,8},{8,16},{16,24},{25,1},{1,9},{9,17},{17,25},{26,2},{2,... | collective-permute-start | bytes 3932168 | tf_op jit(solution)/shard_map/ppermute | solution.py:433
  5.5 0.0 copy-start.8
  5.5 1.2 %copy-done.8 = bf16[4,128,896]{2,1,0:T(8,128)(2,1)S(1)} copy-done((bf16[4,128,896]{2,1,0:T(8,128)(2,1)S(1)}, bf16[4,128,896]{2,1,0:T(8,128)(2,1)}, u32[]{:S(2)}) %copy-start.8) | copy-done | bytes 917528
  6.6 0.0 copy-start.9
  6.6 0.7 copy-done.9
  7.3 0.0 copy-start.12
  7.3 0.0 copy-start.13
  7.3 8.9 %encode_rows.1.refs_4_ = bf16[4,128,896]{2,1,0:T(8,128)(2,1)} custom-call(bf16[4,128,896]{2,1,0:T(8,128)(2,1)S(1)} %copy-done.8, f32[1,896]{1,0:T(1,128)S(1)} %copy-done.9, bf16[1,896,2688]{2,1,0:T(8,128)(2,1)} %wqkv_hbm.1, bf16[1,896,896]{2,1,0:T(8,128)(2,1)} %wout_hbm.1), custom_call_target="tpu_custom_call" | custom-call | flops 8000000000 | bytes 1 | tf_op jit(solution)/shard_map/encode_rows/pallas_call | solution.py:97
  16.3 0.1 collective-permute-start
  16.3 1.6 %collective-permute-start.2 = (bf16[4,128,896]{2,1,0:T(8,128)(2,1)}, bf16[4,128,896]{2,1,0:T(8,128)(2,1)S(1)}, u32[]{:S(2)}, u32[]{:S(2)}) collective-permute-start(bf16[4,128,896]{2,1,0:T(8,128)(2,1)} %encode_rows.1.refs_4_), channel_id=1, source_target_pairs={{0,4},{1,5},{2,6},{3,7},{4,0},{5,1},{6,2},{7,3},{8,12},{9,13},{10,... | collective-permute-start | bytes 2752520 | tf_op jit(solution)/shard_map/ppermute | solution.py:438
  17.9 1.5 %collective-permute-start.1 = (bf16[4,128,896]{2,1,0:T(8,128)(2,1)}, bf16[4,128,896]{2,1,0:T(8,128)(2,1)S(1)}, u32[]{:S(2)}, u32[]{:S(2)}) collective-permute-start(bf16[4,128,896]{2,1,0:T(8,128)(2,1)} %encode_rows.1.refs_4_), channel_id=1, source_target_pairs={{0,2},{1,3},{2,0},{3,1},{4,6},{5,7},{6,4},{7,5},{8,10},{9,11},{10,... | collective-permute-start | bytes 2752520 | tf_op jit(solution)/shard_map/ppermute | solution.py:438
  19.4 0.0 copy-done.12
  19.4 0.7 copy.19.refs_0_
  20.1 0.0 copy-done.13
  20.1 0.7 copy.20.refs_1_
  20.8 0.0 collective-permute-done.refs_5_
  20.8 0.0 copy-start.4
  20.8 11.0 %keyvals_rows.2 = (bf16[14,128,4096]{2,1,0:T(8,128)(2,1)}, bf16[896,4096]{1,0:T(8,128)(2,1)S(1)}, f32[8,128]{1,0:T(8,128)}) custom-call(s32[1,7,2]{2,1,0:T(8,128)} %copy.19.refs_0_, s32[1,7,2]{2,1,0:T(8,128)} %copy.20.refs_1_, s32[1]{0:T(128)} %bitcast.refs_2_, bf16[1,896,4096]{2,1,0:T(8,128)(2,1)} %refs_3_.1, bf16[4,128,896]{2,1,0:T(8,128)(2,1)} %encode_rows.1.refs_4_, ...), custom_call_target="tpu_custom_call" | custom-call | flops 4000000000 | bytes 1 | tf_op jit(solution)/shard_map/keyvals_rows/pallas_call | solution.py:215
  31.8 7.6 %collective-permute-done.2.y_ref = bf16[4,128,896]{2,1,0:T(8,128)(2,1)S(1)} collective-permute-done((bf16[4,128,896]{2,1,0:T(8,128)(2,1)}, bf16[4,128,896]{2,1,0:T(8,128)(2,1)S(1)}, u32[]{:S(2)}, u32[]{:S(2)}) %collective-permute-start.2) | collective-permute-done | bytes 917536 | tf_op jit(solution)/shard_map/ppermute | solution.py:438
  39.3 1.2 %collective-permute-done.1.x_ref = bf16[4,128,896]{2,1,0:T(8,128)(2,1)S(1)} collective-permute-done((bf16[4,128,896]{2,1,0:T(8,128)(2,1)}, bf16[4,128,896]{2,1,0:T(8,128)(2,1)S(1)}, u32[]{:S(2)}, u32[]{:S(2)}) %collective-permute-start.1) | collective-permute-done | bytes 917536 | tf_op jit(solution)/shard_map/ppermute | solution.py:438
  40.5 0.0 collective-permute-done.3.done_ref.refs_5_
  40.5 0.0 copy-done.4
  40.6 0.0 copy-start.7
  40.6 0.7 copy-done.7
  41.2 1.4 %next_sends.1 = (bf16[2,128,896]{2,1,0:T(8,128)(2,1)S(1)}, bf16[2,128,896]{2,1,0:T(8,128)(2,1)S(1)}, bf16[1,128,2048]{2,1,0:T(8,128)(2,1)}, bf16[4,128,896]{2,1,0:T(8,128)(2,1)S(1)}, bf16[4,128,896]{2,1,0:T(8,128)(2,1)S(1)}) custom-call(bf16[4,128,896]{2,1,0:T(8,128)(2,1)S(1)} %collective-permute-done.1.x_ref, ...), custom_call_target="tpu_custom_call", output_to_operand_aliasing={{3}: (0, {}), {4}: (1, {})} | custom-call | flops 1000000000 | bytes 1 | tf_op jit(solution)/shard_map/next_sends/pallas_call | solution.py:396
  42.7 0.0 copy-start.2
  42.7 0.0 copy-start.3
  42.7 0.1 collective-permute-start.4
  42.8 0.5 collective-permute-start.5
  43.3 0.5 collective-permute-start.7
  43.8 1.5 %collective-permute-start.8 = (bf16[2,128,896]{2,1,0:T(8,128)(2,1)S(1)}, bf16[2,128,896]{2,1,0:T(8,128)(2,1)}, u32[]{:S(2)}, u32[]{:S(2)}) collective-permute-start(bf16[2,128,896]{2,1,0:T(8,128)(2,1)S(1)} %get-tuple-element.27), channel_id=1, source_target_pairs={{0,2},{1,3},{2,0},{3,1},{4,6},{5,7},{6,4},{7,5},{8,10},{9,11},{10,... | collective-permute-start | bytes 1376264 | tf_op jit(solution)/shard_map/ppermute | solution.py:438
  45.3 1.6 %collective-permute-start.6 = (bf16[1,128,2048]{2,1,0:T(8,128)(2,1)}, bf16[1,128,2048]{2,1,0:T(8,128)(2,1)}, u32[]{:S(2)}, u32[]{:S(2)}) collective-permute-start(bf16[1,128,2048]{2,1,0:T(8,128)(2,1)} %get-tuple-element.25), channel_id=1, source_target_pairs={{24,0},{0,8},{8,16},{16,24},{25,1},{1,9},{9,17},{17,25},{26,2},{2,... | collective-permute-start | bytes 1572872 | tf_op jit(solution)/shard_map/ppermute | solution.py:433
  46.8 0.0 collective-permute-done.4.refs_5_
  46.8 0.0 copy-start.10
  46.8 0.0 collective-permute-done.5.refs_7_
  46.8 0.0 copy-start.11
  46.9 0.0 copy-done.2
  46.9 0.0 copy-done.3
  46.9 0.9 %copy-done.10 = bf16[4,128,896]{2,1,0:T(8,128)(2,1)} copy-done((bf16[4,128,896]{2,1,0:T(8,128)(2,1)}, bf16[4,128,896]{2,1,0:T(8,128)(2,1)S(1)}, u32[]{:S(2)}) %copy-start.10) | copy-done | bytes 917528
  47.8 0.3 copy-done.11
  48.0 0.0 copy-start.5
  48.1 0.0 copy-start.6
  48.1 13.2 %keyvals_rows.3 = (bf16[14,128,4096]{2,1,0:T(8,128)(2,1)}, bf16[896,4096]{1,0:T(8,128)(2,1)S(1)}, f32[8,128]{1,0:T(8,128)}) custom-call(s32[1,7,2]{2,1,0:T(8,128)} %copy.19.refs_0_, s32[1,7,2]{2,1,0:T(8,128)} %copy.20.refs_1_, s32[1]{0:T(128)} %bitcast.refs_2_, ...), custom_call_target="tpu_custom_call", output_to_operand_aliasing={{1}: (3, {}), {0}: (8, {})} | custom-call | flops 4000000000 | bytes 1 | tf_op jit(solution)/shard_map/keyvals_rows/pallas_call | solution.py:215
  61.2 0.0 copy-start
  61.2 3.0 %copy-done = bf16[896,4096]{1,0:T(8,128)(2,1)} copy-done((bf16[896,4096]{1,0:T(8,128)(2,1)}, bf16[896,4096]{1,0:T(8,128)(2,1)S(1)}, u32[]{:S(2)}) %copy-start) | copy-done | bytes 7340056
  64.2 0.0 collective-permute-done.7.low_ref
  64.2 0.0 collective-permute-done.8.high_ref
  64.2 0.0 collective-permute-start.9
  64.2 0.5 collective-permute-start.10
  64.7 0.0 collective-permute-done.6.refs_6_
  64.7 1.5 %collective-permute-done.9.refs_8_ = bf16[2,128,896]{2,1,0:T(8,128)(2,1)S(1)} collective-permute-done((bf16[2,128,896]{2,1,0:T(8,128)(2,1)}, bf16[2,128,896]{2,1,0:T(8,128)(2,1)S(1)}, u32[]{:S(2)}, u32[]{:S(2)}) %collective-permute-start.9) | collective-permute-done | bytes 458784 | tf_op jit(solution)/shard_map/ppermute | solution.py:438
  66.2 0.7 collective-permute-done.10.refs_10_
  66.9 0.0 copy-done.5
  66.9 0.0 copy-done.6
  66.9 0.0 copy-start.1
  66.9 3.1 %copy-done.1 = bf16[896,4096]{1,0:T(8,128)(2,1)S(1)} copy-done((bf16[896,4096]{1,0:T(8,128)(2,1)S(1)}, bf16[896,4096]{1,0:T(8,128)(2,1)}, u32[]{:S(2)}) %copy-start.1) | copy-done | bytes 7340056
  70.0 13.9 %attend_spans.1 = bf16[1,448,2048]{2,1,0:T(8,128)(2,1)} custom-call(s32[1,7,2]{2,1,0:T(8,128)S(1)} %copy-done.5, s32[1,7,2]{2,1,0:T(8,128)S(1)} %copy-done.6, s32[1]{0:T(128)} %bitcast.refs_2_, bf16[896,4096]{1,0:T(8,128)(2,1)S(1)} %copy-done.1, bf16[14,128,4096]{2,1,0:T(8,128)(2,1)} %get-tuple-element.24.refs_4_, ...), custom_call_target="tpu_custom_call" | custom-call | flops 6000000000 | bytes 1 | tf_op jit(solution)/shard_map/attend_spans/pallas_call | solution.py:338
  (1 shorter events, 0.0 us)
Async XLA Ops:
  2.4 38.2 %collective-permute-start.3 = (bf16[1,320,2048]{2,1,0:T(8,128)(2,1)}, bf16[1,320,2048]{2,1,0:T(8,128)(2,1)S(1)}, u32[]{:S(2)}, u32[]{:S(2)}) collective-permute-start(bf16[1,320,2048]{2,1,0:T(8,128)(2,1)} %first_queries.1), channel_id=1, source_target_pairs={{24,0},{0,8},{8,16},{16,24},{25,1},{1,9},{9,17},{17,25},{26,2},{2,... | collective-permute-start | bytes 3932168 | tf_op jit(solution)/shard_map/ppermute | solution.py:433
  5.5 1.2 %copy-start.8 = (bf16[4,128,896]{2,1,0:T(8,128)(2,1)S(1)}, bf16[4,128,896]{2,1,0:T(8,128)(2,1)}, u32[]{:S(2)}) copy-start(bf16[4,128,896]{2,1,0:T(8,128)(2,1)} %rows_ref.1) | copy-start | bytes 2752516
  6.6 0.7 copy-start.9
  7.3 12.1 %copy-start.12 = (s32[1,7,2]{1,2,0:T(2,128)S(1)}, s32[1,7,2]{1,2,0:T(2,128)}, u32[]{:S(2)}) copy-start(s32[1,7,2]{1,2,0:T(2,128)} %param.10) | copy-start | bytes 172
  7.3 12.7 %copy-start.13 = (s32[1,7,2]{1,2,0:T(2,128)S(1)}, s32[1,7,2]{1,2,0:T(2,128)}, u32[]{:S(2)}) copy-start(s32[1,7,2]{1,2,0:T(2,128)} %param.11) | copy-start | bytes 172
  16.3 4.5 %collective-permute-start = (bf16[4,128,896]{2,1,0:T(8,128)(2,1)}, bf16[4,128,896]{2,1,0:T(8,128)(2,1)}, u32[]{:S(2)}, u32[]{:S(2)}) collective-permute-start(bf16[4,128,896]{2,1,0:T(8,128)(2,1)} %encode_rows.1.refs_4_), channel_id=1, source_target_pairs={{0,1},{1,0},{2,3},{3,2},{4,5},{5,4},{6,7},{7,6},{8,9},{9,8},{10,11... | collective-permute-start | bytes 2752520 | tf_op jit(solution)/shard_map/ppermute | solution.py:438
  16.3 23.0 %collective-permute-start.2 = (bf16[4,128,896]{2,1,0:T(8,128)(2,1)}, bf16[4,128,896]{2,1,0:T(8,128)(2,1)S(1)}, u32[]{:S(2)}, u32[]{:S(2)}) collective-permute-start(bf16[4,128,896]{2,1,0:T(8,128)(2,1)} %encode_rows.1.refs_4_), channel_id=1, source_target_pairs={{0,4},{1,5},{2,6},{3,7},{4,0},{5,1},{6,2},{7,3},{8,12},{9,13},{10,... | collective-permute-start | bytes 2752520 | tf_op jit(solution)/shard_map/ppermute | solution.py:438
  17.9 22.6 %collective-permute-start.1 = (bf16[4,128,896]{2,1,0:T(8,128)(2,1)}, bf16[4,128,896]{2,1,0:T(8,128)(2,1)S(1)}, u32[]{:S(2)}, u32[]{:S(2)}) collective-permute-start(bf16[4,128,896]{2,1,0:T(8,128)(2,1)} %encode_rows.1.refs_4_), channel_id=1, source_target_pairs={{0,2},{1,3},{2,0},{3,1},{4,6},{5,7},{6,4},{7,5},{8,10},{9,11},{10,... | collective-permute-start | bytes 2752520 | tf_op jit(solution)/shard_map/ppermute | solution.py:438
  20.8 19.8 %copy-start.4 = (bf16[1,448,2048]{2,1,0:T(8,128)(2,1)S(1)}, bf16[1,448,2048]{2,1,0:T(8,128)(2,1)}, u32[]{:S(2)}) copy-start(bf16[1,448,2048]{2,1,0:T(8,128)(2,1)} %q_ref.3) | copy-start | bytes 5505028
  40.6 0.7 copy-start.7
  42.7 4.2 %copy-start.2 = (bf16[4,128,896]{2,1,0:T(8,128)(2,1)}, bf16[4,128,896]{2,1,0:T(8,128)(2,1)S(1)}, u32[]{:S(2)}) copy-start(bf16[4,128,896]{2,1,0:T(8,128)(2,1)S(1)} %get-tuple-element.21.refs_6_) | copy-start | bytes 2752516
  42.7 4.2 %copy-start.3 = (bf16[4,128,896]{2,1,0:T(8,128)(2,1)}, bf16[4,128,896]{2,1,0:T(8,128)(2,1)S(1)}, u32[]{:S(2)}) copy-start(bf16[4,128,896]{2,1,0:T(8,128)(2,1)S(1)} %get-tuple-element.20.refs_4_) | copy-start | bytes 2752516
  42.7 4.2 %collective-permute-start.4 = (bf16[4,128,896]{2,1,0:T(8,128)(2,1)S(1)}, bf16[4,128,896]{2,1,0:T(8,128)(2,1)S(1)}, u32[]{:S(2)}, u32[]{:S(2)}) collective-permute-start(bf16[4,128,896]{2,1,0:T(8,128)(2,1)S(1)} %get-tuple-element.20.refs_4_), channel_id=1, source_target_pairs={{0,1},{1,0},{2,3},{3,2},{4,5},{5,4},{6,7},{7,6},{8,9},{9,8},{10,11... | collective-permute-start | bytes 2752520 | tf_op jit(solution)/shard_map/ppermute | solution.py:438
  42.8 4.1 %collective-permute-start.5 = (bf16[4,128,896]{2,1,0:T(8,128)(2,1)S(1)}, bf16[4,128,896]{2,1,0:T(8,128)(2,1)S(1)}, u32[]{:S(2)}, u32[]{:S(2)}) collective-permute-start(bf16[4,128,896]{2,1,0:T(8,128)(2,1)S(1)} %get-tuple-element.21.refs_6_), channel_id=1, source_target_pairs={{0,1},{1,0},{2,3},{3,2},{4,5},{5,4},{6,7},{7,6},{8,9},{9,8},{10,11... | collective-permute-start | bytes 2752520 | tf_op jit(solution)/shard_map/ppermute | solution.py:438
  43.3 20.9 %collective-permute-start.7 = (bf16[2,128,896]{2,1,0:T(8,128)(2,1)S(1)}, bf16[2,128,896]{2,1,0:T(8,128)(2,1)}, u32[]{:S(2)}, u32[]{:S(2)}) collective-permute-start(bf16[2,128,896]{2,1,0:T(8,128)(2,1)S(1)} %get-tuple-element.26), channel_id=1, source_target_pairs={{0,4},{1,5},{2,6},{3,7},{4,0},{5,1},{6,2},{7,3},{8,12},{9,13},{10,... | collective-permute-start | bytes 1376264 | tf_op jit(solution)/shard_map/ppermute | solution.py:438
  43.8 20.4 %collective-permute-start.8 = (bf16[2,128,896]{2,1,0:T(8,128)(2,1)S(1)}, bf16[2,128,896]{2,1,0:T(8,128)(2,1)}, u32[]{:S(2)}, u32[]{:S(2)}) collective-permute-start(bf16[2,128,896]{2,1,0:T(8,128)(2,1)S(1)} %get-tuple-element.27), channel_id=1, source_target_pairs={{0,2},{1,3},{2,0},{3,1},{4,6},{5,7},{6,4},{7,5},{8,10},{9,11},{10,... | collective-permute-start | bytes 1376264 | tf_op jit(solution)/shard_map/ppermute | solution.py:438
  45.3 19.5 %collective-permute-start.6 = (bf16[1,128,2048]{2,1,0:T(8,128)(2,1)}, bf16[1,128,2048]{2,1,0:T(8,128)(2,1)}, u32[]{:S(2)}, u32[]{:S(2)}) collective-permute-start(bf16[1,128,2048]{2,1,0:T(8,128)(2,1)} %get-tuple-element.25), channel_id=1, source_target_pairs={{24,0},{0,8},{8,16},{16,24},{25,1},{1,9},{9,17},{17,25},{26,2},{2,... | collective-permute-start | bytes 1572872 | tf_op jit(solution)/shard_map/ppermute | solution.py:433
  46.8 0.9 %copy-start.10 = (bf16[4,128,896]{2,1,0:T(8,128)(2,1)}, bf16[4,128,896]{2,1,0:T(8,128)(2,1)S(1)}, u32[]{:S(2)}) copy-start(bf16[4,128,896]{2,1,0:T(8,128)(2,1)S(1)} %collective-permute-done.4.refs_5_) | copy-start | bytes 2752516
  46.8 1.2 %copy-start.11 = (bf16[4,128,896]{2,1,0:T(8,128)(2,1)}, bf16[4,128,896]{2,1,0:T(8,128)(2,1)S(1)}, u32[]{:S(2)}) copy-start(bf16[4,128,896]{2,1,0:T(8,128)(2,1)S(1)} %collective-permute-done.5.refs_7_) | copy-start | bytes 2752516
  48.0 18.8 %copy-start.5 = (s32[1,7,2]{2,1,0:T(8,128)S(1)}, s32[1,7,2]{2,1,0:T(8,128)}, u32[]{:S(2)}) copy-start(s32[1,7,2]{2,1,0:T(8,128)} %copy.19.refs_0_) | copy-start | bytes 172
  48.1 18.8 %copy-start.6 = (s32[1,7,2]{2,1,0:T(8,128)S(1)}, s32[1,7,2]{2,1,0:T(8,128)}, u32[]{:S(2)}) copy-start(s32[1,7,2]{2,1,0:T(8,128)} %copy.20.refs_1_) | copy-start | bytes 172
  61.2 3.0 %copy-start = (bf16[896,4096]{1,0:T(8,128)(2,1)}, bf16[896,4096]{1,0:T(8,128)(2,1)S(1)}, u32[]{:S(2)}) copy-start(bf16[896,4096]{1,0:T(8,128)(2,1)S(1)} %get-tuple-element.23.refs_3_) | copy-start | bytes 22020100
  64.2 2.0 %collective-permute-start.9 = (bf16[2,128,896]{2,1,0:T(8,128)(2,1)}, bf16[2,128,896]{2,1,0:T(8,128)(2,1)S(1)}, u32[]{:S(2)}, u32[]{:S(2)}) collective-permute-start(bf16[2,128,896]{2,1,0:T(8,128)(2,1)} %get-tuple-element.29.refs_7_), channel_id=1, source_target_pairs={{0,1},{1,0},{2,3},{3,2},{4,5},{5,4},{6,7},{7,6},{8,9},{9,8},{10,11... | collective-permute-start | bytes 1376264 | tf_op jit(solution)/shard_map/ppermute | solution.py:438
  64.2 2.7 %collective-permute-start.10 = (bf16[2,128,896]{2,1,0:T(8,128)(2,1)}, bf16[2,128,896]{2,1,0:T(8,128)(2,1)S(1)}, u32[]{:S(2)}, u32[]{:S(2)}) collective-permute-start(bf16[2,128,896]{2,1,0:T(8,128)(2,1)} %get-tuple-element.30.refs_9_), channel_id=1, source_target_pairs={{0,1},{1,0},{2,3},{3,2},{4,5},{5,4},{6,7},{7,6},{8,9},{9,8},{10,11... | collective-permute-start | bytes 1376264 | tf_op jit(solution)/shard_map/ppermute | solution.py:438
  66.9 3.1 %copy-start.1 = (bf16[896,4096]{1,0:T(8,128)(2,1)S(1)}, bf16[896,4096]{1,0:T(8,128)(2,1)}, u32[]{:S(2)}) copy-start(bf16[896,4096]{1,0:T(8,128)(2,1)} %copy-done) | copy-start | bytes 22020100

commit v2 on v1

--- a/solution.py
+++ b/solution.py
@@ -19,6 +19,7 @@
 VM = pl.BlockSpec(memory_space=pltpu.VMEM)
 SM = pl.BlockSpec(memory_space=pltpu.SMEM)
 EARLY = 5
+PER = 1024
 E_US, KV_US, CROSS_US = 8.0, 4.0, 6.0
 
 
@@ -106,18 +107,17 @@
             pltpu.VMEM((tokens, width), BF),
             pltpu.SemaphoreType.DMA((13,)),
         ],
-        compiler_params=pltpu.CompilerParams(vmem_limit_bytes=52 * MB),
+        compiler_params=pltpu.CompilerParams(vmem_limit_bytes=58 * MB),
         cost_estimate=cost(E_US),
         name="encode_rows",
     )(rows, gain, w_qkv, w_out)
 
 
-def gather_rows(plan, sources, owner_ref, row_ref, me, rows, slots, sems, taken):
-    spans, picks = owner_ref.shape[1:]
+def gather_rows(plan, sources, ids_ref, me, rows, slots, sems, taken):
 
     def look(s, found):
-        owner = owner_ref[0, s // picks, lax.rem(s, picks)]
-        row = row_ref[0, s // picks, lax.rem(s, picks)]
+        code = ids_ref[s]
+        owner, row = lax.shift_right_logical(code, 10), jnp.bitwise_and(code, PER - 1)
         if taken is not None:
             taken[s] = 0
         for source, test, place in plan(sources, owner, jnp.bitwise_xor(owner, me), row):
@@ -132,10 +132,10 @@
             found = found + test.astype(jnp.int32)
         return found
 
-    return lax.fori_loop(0, spans * picks, look, jnp.int32(0))
-
-
-def project_pairs(found, source, w_ref, rows, sems, finish, after):
+    return lax.fori_loop(0, ids_ref.shape[0], look, jnp.int32(0))
+
+
+def project_pairs(found, source, w_ref, rows, sems, finish):
     length, width = rows.shape[1:]
     chunk = 1024
 
@@ -152,15 +152,14 @@
             cols = pl.ds(b * chunk, chunk)
             out = jnp.dot(both, w_ref[:, cols], preferred_element_type=F32).astype(BF)
             finish(i, cols, out[:length], out[length:])
-        after(i)
         return carry
 
     lax.fori_loop(0, (found + 1) // 2, project, 0)
 
 
 def kv_kernel(plan, n_src, fresh, *refs):
-    owner_ref, row_ref, me_ref, w_in = refs[:4]
-    sources = refs[4 : 4 + n_src]
+    ids_ref, me_ref, w_in = refs[:3]
+    sources = refs[3 : 3 + n_src]
     kv_hbm, w_ref, token_ref, rows, made, slots, sems, w_sem, out_sems = refs[-9:]
     if fresh:
         step = w_ref.shape[0] // 8
@@ -170,7 +169,7 @@
         ]
         for load in loads:
             load.start()
-    found = gather_rows(plan, sources, owner_ref, row_ref, me_ref[0], rows, slots, sems, None)
+    found = gather_rows(plan, sources, ids_ref, me_ref[0], rows, slots, sems, None)
     if fresh:
         for load in loads:
             load.wait()
@@ -178,38 +177,39 @@
     def store(i):
         return pltpu.make_async_copy(made.at[i], kv_hbm.at[slots[i]], out_sems.at[i])
 
+    def send(i, cols):
+        pltpu.make_async_copy(made.at[i, :, cols], kv_hbm.at[slots[i], :, cols], out_sems.at[i]).start()
+
     def finish(i, cols, one, two):
         made[i, :, cols] = one
         made[i + 1, :, cols] = two
-
-    def send(i):
-        store(i).start()
+        send(i, cols)
 
         @pl.when(i + 1 < found)
         def _():
-            store(i + 1).start()
+            send(i + 1, cols)
 
     def drain(i, carry):
         store(i).wait()
         return carry
 
-    project_pairs(found, sources[0], w_ref, rows, sems, finish, send)
+    project_pairs(found, sources[0], w_ref, rows, sems, finish)
     lax.fori_loop(0, found, drain, 0)
     token_ref[...] = jnp.zeros_like(token_ref)
 
 
-def keyvals_part(owner, row, me, sources, w_kv, before, plan, most):
+def keyvals_part(ids, me, sources, w_kv, before, plan, most):
     length, width = sources[0].shape[1:]
     features = w_kv.shape[-1]
-    slots = owner.shape[1] * owner.shape[2]
+    slots = ids.shape[0]
     most = min(most, slots)
     most += most % 2
     fresh = before is None
-    operands = [owner, row, me, w_kv, *sources]
-    specs = [SM, SM, SM, ANY if fresh else VM] + [ANY] * len(sources)
+    operands = [ids, me, w_kv, *sources]
+    specs = [SM, SM, ANY if fresh else VM] + [ANY] * len(sources)
     aliases = {}
     if not fresh:
-        aliases = {3: 1, len(operands): 0}
+        aliases = {2: 1, len(operands): 0}
         operands.append(before)
         specs.append(ANY)
     return pl.pallas_call(
@@ -217,7 +217,7 @@
         out_shape=[
             jax.ShapeDtypeStruct((slots, length, features), BF),
             pltpu.VMEM((width, features), BF),
-            jax.ShapeDtypeStruct((8, 128), F32),
+            pltpu.VMEM((8, 128), F32),
         ],
         in_specs=specs,
         out_specs=[ANY, VM, VM],
@@ -267,14 +267,14 @@
 
 
 def final_kernel(plan, n_src, *refs):
-    owner_ref, row_ref, me_ref, w_ref, kv_hbm, first_hbm, second_hbm = refs[:7]
-    sources = refs[7 : 7 + n_src]
-    out_hbm, rows, keyvals, queries, result, slots, taken, sems, kv_sems, q_sems, out_sems = refs[7 + n_src :]
+    ids_ref, me_ref, w_ref, kv_hbm, first_hbm, second_hbm = refs[:6]
+    sources = refs[6 : 6 + n_src]
+    out_hbm, rows, keyvals, queries, result, slots, taken, sems, kv_sems, q_sems, out_sems = refs[6 + n_src :]
     cut = first_hbm.shape[1]
     tokens = queries.shape[0]
-    picks = owner_ref.shape[2]
-    total = owner_ref.shape[1] * picks
-    found = gather_rows(plan, sources, owner_ref, row_ref, me_ref[0], rows, slots, sems, taken)
+    total = ids_ref.shape[0]
+    picks = total * SPAN // tokens
+    found = gather_rows(plan, sources, ids_ref, me_ref[0], rows, slots, sems, taken)
     loads = [
         pltpu.make_async_copy(first_hbm.at[0], queries.at[pl.ds(0, cut)], q_sems.at[0]),
         pltpu.make_async_copy(second_hbm.at[0], queries.at[pl.ds(cut, tokens - cut)], q_sems.at[1]),
@@ -302,7 +302,7 @@
             keyvals[slots[i + 1], :, cols] = two
 
     if n_src:
-        project_pairs(found, sources[0], w_ref, rows, sems, finish, lambda i: None)
+        project_pairs(found, sources[0], w_ref, rows, sems, finish)
     for load in loads:
         load.wait()
 
@@ -331,14 +331,14 @@
     lax.fori_loop(0, tokens // SPAN, drain, 0)
 
 
-def final(owner, row, me, sources, w, kv, first, second, plan, most):
+def final(ids, me, sources, w, kv, first, second, plan, most):
     length, width = kv.shape[1], w.shape[0]
-    slots = owner.shape[1] * owner.shape[2]
+    slots = ids.shape[0]
     tokens, features = first.shape[1] + second.shape[1], first.shape[2]
     return pl.pallas_call(
         functools.partial(final_kernel, plan, len(sources)),
         out_shape=jax.ShapeDtypeStruct((1, tokens, features), BF),
-        in_specs=[SM, SM, SM, VM] + [ANY] * (3 + len(sources)),
+        in_specs=[SM, SM, VM] + [ANY] * (3 + len(sources)),
         out_specs=ANY,
         scratch_shapes=[
             pltpu.VMEM((most, length, width), BF),
@@ -355,13 +355,20 @@
         compiler_params=pltpu.CompilerParams(vmem_limit_bytes=36 * MB),
         cost_estimate=cost(CROSS_US),
         name="attend_spans",
-    )(owner, row, me, w, kv, first, second, *sources)
-
-
-def head_kernel(q_ref, out_ref, sem):
-    copy = pltpu.make_async_copy(q_ref.at[:, pl.ds(0, out_ref.shape[1])], out_ref, sem)
-    copy.start()
-    copy.wait()
+    )(ids, me, w, kv, first, second, *sources)
+
+
+def head_kernel(q_ref, out_ref, sems):
+    count = sems.shape[0]
+    step = out_ref.shape[1] // count
+    copies = [
+        pltpu.make_async_copy(q_ref.at[:, pl.ds(i * step, step)], out_ref.at[:, pl.ds(i * step, step)], sems.at[i])
+        for i in range(count)
+    ]
+    for copy in copies:
+        copy.start()
+    for copy in copies:
+        copy.wait()
 
 
 def head(queries, count):
@@ -370,14 +377,16 @@
         out_shape=pltpu.VMEM((1, count, queries.shape[2]), BF),
         in_specs=[ANY],
         out_specs=VM,
-        scratch_shapes=[pltpu.SemaphoreType.DMA],
+        scratch_shapes=[pltpu.SemaphoreType.DMA((count // SPAN,))],
         compiler_params=pltpu.CompilerParams(vmem_limit_bytes=56 * MB),
         cost_estimate=cost(1.0),
         name="first_queries",
     )(queries)
 
 
-def split_kernel(start, x_ref, y_ref, q_ref, done_ref, token_ref, low_ref, high_ref, out_ref, x_out, y_out, sems):
+def split_kernel(
+    start, x_ref, y_ref, q_ref, done_ref, token_ref, low_ref, high_ref, out_ref, x_out, y_out, sems
+):
     half = low_ref.shape[0]
     copies = [
         pltpu.make_async_copy(x_ref.at[pl.ds(0, half)], low_ref, sems.at[0]),
@@ -420,9 +429,10 @@
     return pl.pallas_call(
         relay_kernel,
         out_shape=[jax.ShapeDtypeStruct(low.shape, BF), jax.ShapeDtypeStruct(high.shape, BF)],
-        in_specs=[ANY, ANY, ANY],
+        in_specs=[ANY, ANY, VM],
         out_specs=[ANY, ANY],
         input_output_aliases={0: 0, 1: 1},
+        compiler_params=pltpu.CompilerParams(vmem_limit_bytes=MB),
         cost_estimate=cost(0.1),
         name="after_rows",
     )(low, high, token)
@@ -446,23 +456,27 @@
     start = EARLY * spans // 7 * SPAN
     first = shifted(head(query_states, start))
     me = lax.axis_index("dp").astype(jnp.int32).reshape(1)
+    ids = (nb_owner * PER + nb_row).reshape(-1)
     own = encode(cache_emb, enc_gain, w_qkv, w_out)
-    part = functools.partial(keyvals_part, nb_owner, nb_row, me)
+    part = functools.partial(keyvals_part, ids, me)
     if dp == 8 and per % 2 == 0:
         half = per // 2
-        x, y, near = swapped(own, 2), swapped(own, 4), swapped(own, 1)
-        kv, w, token = part([own, near], w_kv, None, lambda src, owner, hop, row: [(src[i], hop == i, row) for i in range(2)], 4)
-        xl, yh, rest, x, y = split(x, y, query_states, start, first, token)
-        dl, dh, second = swapped(xl, 4), swapped(yh, 2), shifted(rest)
-        xs, ys = swapped(x, 1), swapped(y, 1)
-        kv, w, token = part(
-            [x, xs, y, ys], w, kv, lambda src, owner, hop, row: [(src[i], hop == i + 2, row) for i in range(4)], 8
-        )
+
+        def nearest(src, owner, hop, row):
+            return [(src[i], hop == i, row) for i in range(2)]
+
+        def middle(src, owner, hop, row):
+            return [(src[i], hop == i + 2, row) for i in range(4)]
 
         def last(src, owner, hop, row):
             lows = [(src[i], (hop == i + 6) & (row < half), row) for i in range(2)]
             return lows + [(src[i + 2], (hop == i + 6) & (row >= half), row - half) for i in range(2)]
 
+        x, y, near = swapped(own, 2), swapped(own, 4), swapped(own, 1)
+        kv, w, token = part([own, near], w_kv, None, nearest, 4)
+        xl, yh, rest, x, y = split(x, y, query_states, start, first, token)
+        dl, dh, second = swapped(xl, 4), swapped(yh, 2), shifted(rest)
+        kv, w, token = part([x, swapped(x, 1), y, swapped(y, 1)], w, kv, middle, 8)
         dl, dh = relay(dl, dh, token)
         sources = [dl, swapped(dl, 1), dh, swapped(dh, 1)]
     else:
@@ -474,7 +488,7 @@
         def last(src, owner, hop, row):
             return []
 
-    return final(nb_owner, nb_row, me, sources, w, kv, first, second, last, 4)
+    return final(ids, me, sources, w, kv, first, second, last, 4)
 
 
 def solution(mesh):

time: 84.3 us -> 73.7 us (0.87)
  local copies, waits for them, and re-layouts: 11.1 us -> 1.93 us
  Pallas kernels: 50.8 us -> 47 us
  waiting for transfers between devices: 11 us -> 12.8 us
    unnamed x30 -> x16, local copies, waits for them, and re-layouts: 11.1 us -> 1.24 us
    pallas_call x2, Pallas kernels: 24.2 us -> 19.6 us  [keyvals_part(): pl.pallas_call(functools.partial(kv_kernel, plan, len(sources), fresh), o...]
    ppermute x2, waiting for transfers between devices: 0.01 us -> 1.75 us  [shifted(): return lax.ppermute(block, 'section', [((i - 1) % n, i) for i in range(n)])]
    pallas_call x1, Pallas kernels: 8.91 us -> 10 us  [encode(): pl.pallas_call(encode_kernel, out_shape=jax.ShapeDtypeStruct(rows.shape,...]
  transfers between devices with their start and end apart: 11 -> 11, of which waited for: 4 -> 4; matrix products, arithmetic and copies ran while one was open for 2% -> 1% of each run, Pallas kernels for 39% -> 41%
where the time goes in v2:
time: 73.7 us; the launch traced here: 72.8 us
  Pallas kernels  47 us (64%)
  waiting for transfers between devices  12.8 us (17%)
  starting transfers between devices  10.9 us (15%)
  local copies, waits for them, and re-layouts  1.93 us (3%)
    pallas_call x2, Pallas kernels, keyvals_part(): pl.pallas_call(functools.partial(kv_kernel, plan, len(sources), fresh), o...  19.6 us
    pallas_call x1, Pallas kernels, final(): pl.pallas_call(functools.partial(final_kernel, plan, len(sources)), out_s...  14.4 us
    ppermute x9, waiting for transfers between devices, swapped(): return lax.ppermute(block, 'dp', [(i, i ^ hop) for i in range(n)])  11 us
    pallas_call x1, Pallas kernels, encode(): pl.pallas_call(encode_kernel, out_shape=jax.ShapeDtypeStruct(rows.shape,...  10 us
    ppermute x9, starting transfers between devices, swapped(): return lax.ppermute(block, 'dp', [(i, i ^ hop) for i in range(n)])  6.27 us
    ppermute x2, starting transfers between devices, shifted(): return lax.ppermute(block, 'section', [((i - 1) % n, i) for i in range(n)])  4.66 us
    pallas_call x1, Pallas kernels, head(): pl.pallas_call(head_kernel, out_shape=pltpu.VMEM((1, count, queries.shape...  2.36 us
    ppermute x2, waiting for transfers between devices, shifted(): return lax.ppermute(block, 'section', [((i - 1) % n, i) for i in range(n)])  1.75 us
  transfers between devices with their start and end apart: 11, of which 4 were waited for; matrix products, arithmetic and copies ran while one was open for 1% of the time, Pallas kernels for 41%

profile of v2, /device:TPU:0, one launch (start us, length us, event | category | flops | bytes accessed | tf_op | source)
XLA Modules:
  0.0 72.8 jit_solution(15654160012192388316)
XLA Ops:
  0.0 2.4 %first_queries.1 = bf16[1,320,2048]{2,1,0:T(8,128)(2,1)} custom-call(bf16[1,448,2048]{2,1,0:T(8,128)(2,1)} %q_ref.3), custom_call_target="tpu_custom_call" | custom-call | flops 1000000000 | bytes 1 | tf_op jit(solution)/shard_map/first_queries/pallas_call | solution.py:375
  2.4 0.0 copy-start.6
  2.4 0.0 copy-start.7
  2.4 3.1 %collective-permute-start.3 = (bf16[1,320,2048]{2,1,0:T(8,128)(2,1)}, bf16[1,320,2048]{2,1,0:T(8,128)(2,1)S(1)}, u32[]{:S(2)}, u32[]{:S(2)}) collective-permute-start(bf16[1,320,2048]{2,1,0:T(8,128)(2,1)} %first_queries.1), channel_id=1, source_target_pairs={{24,0},{0,8},{8,16},{16,24},{25,1},{1,9},{9,17},{17,25},{26,2},{2,... | collective-permute-start | bytes 3932168 | tf_op jit(solution)/shard_map/ppermute | solution.py:443
  5.5 10.0 %encode_rows.1.refs_3_ = bf16[4,128,896]{2,1,0:T(8,128)(2,1)} custom-call(bf16[4,128,896]{2,1,0:T(8,128)(2,1)} %rows_ref.1, f32[1,896]{1,0:T(1,128)} %gain_ref.1, bf16[1,896,2688]{2,1,0:T(8,128)(2,1)} %wqkv_hbm.1, bf16[1,896,896]{2,1,0:T(8,128)(2,1)} %wout_hbm.1), custom_call_target="tpu_custom_call" | custom-call | flops 8000000000 | bytes 1 | tf_op jit(solution)/shard_map/encode_rows/pallas_call | solution.py:98
  15.5 0.1 collective-permute-start
  15.6 1.6 %collective-permute-start.2 = (bf16[4,128,896]{2,1,0:T(8,128)(2,1)}, bf16[4,128,896]{2,1,0:T(8,128)(2,1)S(1)}, u32[]{:S(2)}, u32[]{:S(2)}) collective-permute-start(bf16[4,128,896]{2,1,0:T(8,128)(2,1)} %encode_rows.1.refs_3_), channel_id=1, source_target_pairs={{0,4},{1,5},{2,6},{3,7},{4,0},{5,1},{6,2},{7,3},{8,12},{9,13},{10,... | collective-permute-start | bytes 2752520 | tf_op jit(solution)/shard_map/ppermute | solution.py:448
  17.2 1.5 %collective-permute-start.1 = (bf16[4,128,896]{2,1,0:T(8,128)(2,1)}, bf16[4,128,896]{2,1,0:T(8,128)(2,1)S(1)}, u32[]{:S(2)}, u32[]{:S(2)}) collective-permute-start(bf16[4,128,896]{2,1,0:T(8,128)(2,1)} %encode_rows.1.refs_3_), channel_id=1, source_target_pairs={{0,2},{1,3},{2,0},{3,1},{4,6},{5,7},{6,4},{7,5},{8,10},{9,11},{10,... | collective-permute-start | bytes 2752520 | tf_op jit(solution)/shard_map/ppermute | solution.py:448
  18.7 0.0 copy-done.6
  18.7 0.0 copy-done.7
  18.7 0.1 copy.16
  18.8 0.6 reshape.6.refs_0_
  19.4 0.0 collective-permute-done.refs_4_
  19.4 0.0 copy-start.2
  19.4 9.7 %keyvals_rows.2 = (bf16[14,128,4096]{2,1,0:T(8,128)(2,1)}, bf16[896,4096]{1,0:T(8,128)(2,1)S(1)}, f32[8,128]{1,0:T(8,128)S(1)}) custom-call(s32[14]{0:T(128)} %reshape.6.refs_0_, s32[1]{0:T(128)} %bitcast.refs_1_, bf16[1,896,4096]{2,1,0:T(8,128)(2,1)} %refs_2_.1, bf16[4,128,896]{2,1,0:T(8,128)(2,1)} %encode_rows.1.refs_3_, ...), custom_call_target="tpu_custom_call" | custom-call | flops 4000000000 | bytes 1 | tf_op jit(solution)/shard_map/keyvals_rows/pallas_call | solution.py:215
  29.0 9.5 %collective-permute-done.2.y_ref = bf16[4,128,896]{2,1,0:T(8,128)(2,1)S(1)} collective-permute-done((bf16[4,128,896]{2,1,0:T(8,128)(2,1)}, bf16[4,128,896]{2,1,0:T(8,128)(2,1)S(1)}, u32[]{:S(2)}, u32[]{:S(2)}) %collective-permute-start.2) | collective-permute-done | bytes 917536 | tf_op jit(solution)/shard_map/ppermute | solution.py:448
  38.6 1.2 %collective-permute-done.1.x_ref = bf16[4,128,896]{2,1,0:T(8,128)(2,1)S(1)} collective-permute-done((bf16[4,128,896]{2,1,0:T(8,128)(2,1)}, bf16[4,128,896]{2,1,0:T(8,128)(2,1)S(1)}, u32[]{:S(2)}, u32[]{:S(2)}) %collective-permute-start.1) | collective-permute-done | bytes 917536 | tf_op jit(solution)/shard_map/ppermute | solution.py:448
  39.8 0.0 collective-permute-done.3.done_ref.refs_4_
  39.8 0.0 copy-done.2
  39.8 0.6 next_sends.1
  40.4 0.0 copy-start
  40.4 0.0 copy-start.1
  40.5 0.1 collective-permute-start.4
  40.5 0.5 collective-permute-start.5
  41.0 0.5 collective-permute-start.7
  41.5 1.5 %collective-permute-start.8 = (bf16[2,128,896]{2,1,0:T(8,128)(2,1)S(1)}, bf16[2,128,896]{2,1,0:T(8,128)(2,1)S(1)}, u32[]{:S(2)}, u32[]{:S(2)}) collective-permute-start(bf16[2,128,896]{2,1,0:T(8,128)(2,1)S(1)} %get-tuple-element.27), channel_id=1, source_target_pairs={{0,2},{1,3},{2,0},{3,1},{4,6},{5,7},{6,4},{7,5},{8,10},{9,11},{10,... | collective-permute-start | bytes 1376264 | tf_op jit(solution)/shard_map/ppermute | solution.py:448
  43.0 1.6 %collective-permute-start.6 = (bf16[1,128,2048]{2,1,0:T(8,128)(2,1)S(1)}, bf16[1,128,2048]{2,1,0:T(8,128)(2,1)S(1)}, u32[]{:S(2)}, u32[]{:S(2)}) collective-permute-start(bf16[1,128,2048]{2,1,0:T(8,128)(2,1)S(1)} %get-tuple-element.25), channel_id=1, source_target_pairs={{24,0},{0,8},{8,16},{16,24},{25,1},{1,9},{9,17},{17,25},{26,2},{2,... | collective-permute-start | bytes 1572872 | tf_op jit(solution)/shard_map/ppermute | solution.py:443
  44.6 0.0 collective-permute-done.4.refs_4_
  44.6 0.0 copy-start.4
  44.6 0.0 collective-permute-done.5.refs_6_
  44.6 0.0 copy-start.5
  44.6 0.0 copy-done
  44.6 0.0 copy-done.1
  44.6 0.9 %copy-done.4 = bf16[4,128,896]{2,1,0:T(8,128)(2,1)} copy-done((bf16[4,128,896]{2,1,0:T(8,128)(2,1)}, bf16[4,128,896]{2,1,0:T(8,128)(2,1)S(1)}, u32[]{:S(2)}) %copy-start.4) | copy-done | bytes 917528
  45.5 0.3 copy-done.5
  45.9 0.0 copy-start.3
  45.9 9.9 %keyvals_rows.3 = (bf16[14,128,4096]{2,1,0:T(8,128)(2,1)}, bf16[896,4096]{1,0:T(8,128)(2,1)S(1)}, f32[8,128]{1,0:T(8,128)S(1)}) custom-call(s32[14]{0:T(128)} %reshape.6.refs_0_, s32[1]{0:T(128)} %bitcast.refs_1_, bf16[896,4096]{1,0:T(8,128)(2,1)S(1)} %get-tuple-element.18.refs_2_, ...), custom_call_target="tpu_custom_call", output_to_operand_aliasing={{1}: (2, {}), {0}: (7, {})} | custom-call | flops 4000000000 | bytes 1 | tf_op jit(solution)/shard_map/keyvals_rows/pallas_call | solution.py:215
  55.8 0.0 collective-permute-done.7.low_ref
  55.8 0.0 collective-permute-done.8.high_ref
  55.8 0.1 collective-permute-start.9
  55.9 0.5 collective-permute-start.10
  56.4 1.8 %collective-permute-done.6.refs_5_ = bf16[1,128,2048]{2,1,0:T(8,128)(2,1)S(1)} collective-permute-done((bf16[1,128,2048]{2,1,0:T(8,128)(2,1)S(1)}, bf16[1,128,2048]{2,1,0:T(8,128)(2,1)S(1)}, u32[]{:S(2)}, u32[]{:S(2)}) %collective-permute-start.6) | collective-permute-done | bytes 524320 | tf_op jit(solution)/shard_map/ppermute | solution.py:443
  58.2 0.0 collective-permute-done.9.refs_7_
  58.2 0.2 collective-permute-done.10.refs_9_
  58.4 0.0 copy-done.3
  58.4 14.4 %attend_spans.1 = bf16[1,448,2048]{2,1,0:T(8,128)(2,1)} custom-call(s32[14]{0:T(128)S(1)} %copy-done.3, s32[1]{0:T(128)} %bitcast.refs_1_, bf16[896,4096]{1,0:T(8,128)(2,1)S(1)} %get-tuple-element.23.refs_2_, bf16[14,128,4096]{2,1,0:T(8,128)(2,1)} %get-tuple-element.24.refs_3_, bf16[1,320,2048]{2,1,0:T(8,128)(2,1)S(1)} %collective-permute-done.3.done_ref.refs_4_, ...), custom_call_target="tpu_custom_call" | custom-call | flops 6000000000 | bytes 1 | tf_op jit(solution)/shard_map/attend_spans/pallas_call | solution.py:338
  (2 shorter events, 0.0 us)
Async XLA Ops:
  2.4 16.3 %copy-start.6 = (s32[1,7,2]{1,2,0:T(2,128)S(1)}, s32[1,7,2]{1,2,0:T(2,128)}, u32[]{:S(2)}) copy-start(s32[1,7,2]{1,2,0:T(2,128)} %param.11) | copy-start | bytes 172
  2.4 16.3 %copy-start.7 = (s32[1,7,2]{1,2,0:T(2,128)S(1)}, s32[1,7,2]{1,2,0:T(2,128)}, u32[]{:S(2)}) copy-start(s32[1,7,2]{1,2,0:T(2,128)} %param.10) | copy-start | bytes 172
  2.4 37.4 %collective-permute-start.3 = (bf16[1,320,2048]{2,1,0:T(8,128)(2,1)}, bf16[1,320,2048]{2,1,0:T(8,128)(2,1)S(1)}, u32[]{:S(2)}, u32[]{:S(2)}) collective-permute-start(bf16[1,320,2048]{2,1,0:T(8,128)(2,1)} %first_queries.1), channel_id=1, source_target_pairs={{24,0},{0,8},{8,16},{16,24},{25,1},{1,9},{9,17},{17,25},{26,2},{2,... | collective-permute-start | bytes 3932168 | tf_op jit(solution)/shard_map/ppermute | solution.py:443
  15.5 3.9 %collective-permute-start = (bf16[4,128,896]{2,1,0:T(8,128)(2,1)}, bf16[4,128,896]{2,1,0:T(8,128)(2,1)}, u32[]{:S(2)}, u32[]{:S(2)}) collective-permute-start(bf16[4,128,896]{2,1,0:T(8,128)(2,1)} %encode_rows.1.refs_3_), channel_id=1, source_target_pairs={{0,1},{1,0},{2,3},{3,2},{4,5},{5,4},{6,7},{7,6},{8,9},{9,8},{10,11... | collective-permute-start | bytes 2752520 | tf_op jit(solution)/shard_map/ppermute | solution.py:448
  15.6 23.0 %collective-permute-start.2 = (bf16[4,128,896]{2,1,0:T(8,128)(2,1)}, bf16[4,128,896]{2,1,0:T(8,128)(2,1)S(1)}, u32[]{:S(2)}, u32[]{:S(2)}) collective-permute-start(bf16[4,128,896]{2,1,0:T(8,128)(2,1)} %encode_rows.1.refs_3_), channel_id=1, source_target_pairs={{0,4},{1,5},{2,6},{3,7},{4,0},{5,1},{6,2},{7,3},{8,12},{9,13},{10,... | collective-permute-start | bytes 2752520 | tf_op jit(solution)/shard_map/ppermute | solution.py:448
  17.2 22.6 %collective-permute-start.1 = (bf16[4,128,896]{2,1,0:T(8,128)(2,1)}, bf16[4,128,896]{2,1,0:T(8,128)(2,1)S(1)}, u32[]{:S(2)}, u32[]{:S(2)}) collective-permute-start(bf16[4,128,896]{2,1,0:T(8,128)(2,1)} %encode_rows.1.refs_3_), channel_id=1, source_target_pairs={{0,2},{1,3},{2,0},{3,1},{4,6},{5,7},{6,4},{7,5},{8,10},{9,11},{10,... | collective-permute-start | bytes 2752520 | tf_op jit(solution)/shard_map/ppermute | solution.py:448
  19.4 20.4 %copy-start.2 = (bf16[1,448,2048]{2,1,0:T(8,128)(2,1)S(1)}, bf16[1,448,2048]{2,1,0:T(8,128)(2,1)}, u32[]{:S(2)}) copy-start(bf16[1,448,2048]{2,1,0:T(8,128)(2,1)} %q_ref.3) | copy-start | bytes 5505028
  40.4 4.2 %copy-start = (bf16[4,128,896]{2,1,0:T(8,128)(2,1)}, bf16[4,128,896]{2,1,0:T(8,128)(2,1)S(1)}, u32[]{:S(2)}) copy-start(bf16[4,128,896]{2,1,0:T(8,128)(2,1)S(1)} %get-tuple-element.21.refs_5_) | copy-start | bytes 2752516
  40.4 4.2 %copy-start.1 = (bf16[4,128,896]{2,1,0:T(8,128)(2,1)}, bf16[4,128,896]{2,1,0:T(8,128)(2,1)S(1)}, u32[]{:S(2)}) copy-start(bf16[4,128,896]{2,1,0:T(8,128)(2,1)S(1)} %get-tuple-element.20.refs_3_) | copy-start | bytes 2752516
  40.5 4.2 %collective-permute-start.4 = (bf16[4,128,896]{2,1,0:T(8,128)(2,1)S(1)}, bf16[4,128,896]{2,1,0:T(8,128)(2,1)S(1)}, u32[]{:S(2)}, u32[]{:S(2)}) collective-permute-start(bf16[4,128,896]{2,1,0:T(8,128)(2,1)S(1)} %get-tuple-element.20.refs_3_), channel_id=1, source_target_pairs={{0,1},{1,0},{2,3},{3,2},{4,5},{5,4},{6,7},{7,6},{8,9},{9,8},{10,11... | collective-permute-start | bytes 2752520 | tf_op jit(solution)/shard_map/ppermute | solution.py:448
  40.5 4.1 %collective-permute-start.5 = (bf16[4,128,896]{2,1,0:T(8,128)(2,1)S(1)}, bf16[4,128,896]{2,1,0:T(8,128)(2,1)S(1)}, u32[]{:S(2)}, u32[]{:S(2)}) collective-permute-start(bf16[4,128,896]{2,1,0:T(8,128)(2,1)S(1)} %get-tuple-element.21.refs_5_), channel_id=1, source_target_pairs={{0,1},{1,0},{2,3},{3,2},{4,5},{5,4},{6,7},{7,6},{8,9},{9,8},{10,11... | collective-permute-start | bytes 2752520 | tf_op jit(solution)/shard_map/ppermute | solution.py:448
  41.0 14.8 %collective-permute-start.7 = (bf16[2,128,896]{2,1,0:T(8,128)(2,1)S(1)}, bf16[2,128,896]{2,1,0:T(8,128)(2,1)S(1)}, u32[]{:S(2)}, u32[]{:S(2)}) collective-permute-start(bf16[2,128,896]{2,1,0:T(8,128)(2,1)S(1)} %get-tuple-element.26), channel_id=1, source_target_pairs={{0,4},{1,5},{2,6},{3,7},{4,0},{5,1},{6,2},{7,3},{8,12},{9,13},{10,... | collective-permute-start | bytes 1376264 | tf_op jit(solution)/shard_map/ppermute | solution.py:448
  41.5 14.3 %collective-permute-start.8 = (bf16[2,128,896]{2,1,0:T(8,128)(2,1)S(1)}, bf16[2,128,896]{2,1,0:T(8,128)(2,1)S(1)}, u32[]{:S(2)}, u32[]{:S(2)}) collective-permute-start(bf16[2,128,896]{2,1,0:T(8,128)(2,1)S(1)} %get-tuple-element.27), channel_id=1, source_target_pairs={{0,2},{1,3},{2,0},{3,1},{4,6},{5,7},{6,4},{7,5},{8,10},{9,11},{10,... | collective-permute-start | bytes 1376264 | tf_op jit(solution)/shard_map/ppermute | solution.py:448
  43.0 15.1 %collective-permute-start.6 = (bf16[1,128,2048]{2,1,0:T(8,128)(2,1)S(1)}, bf16[1,128,2048]{2,1,0:T(8,128)(2,1)S(1)}, u32[]{:S(2)}, u32[]{:S(2)}) collective-permute-start(bf16[1,128,2048]{2,1,0:T(8,128)(2,1)S(1)} %get-tuple-element.25), channel_id=1, source_target_pairs={{24,0},{0,8},{8,16},{16,24},{25,1},{1,9},{9,17},{17,25},{26,2},{2,... | collective-permute-start | bytes 1572872 | tf_op jit(solution)/shard_map/ppermute | solution.py:443
  44.6 0.9 %copy-start.4 = (bf16[4,128,896]{2,1,0:T(8,128)(2,1)}, bf16[4,128,896]{2,1,0:T(8,128)(2,1)S(1)}, u32[]{:S(2)}) copy-start(bf16[4,128,896]{2,1,0:T(8,128)(2,1)S(1)} %collective-permute-done.4.refs_4_) | copy-start | bytes 2752516
  44.6 1.2 %copy-start.5 = (bf16[4,128,896]{2,1,0:T(8,128)(2,1)}, bf16[4,128,896]{2,1,0:T(8,128)(2,1)S(1)}, u32[]{:S(2)}) copy-start(bf16[4,128,896]{2,1,0:T(8,128)(2,1)S(1)} %collective-permute-done.5.refs_6_) | copy-start | bytes 2752516
  45.9 12.5 %copy-start.3 = (s32[14]{0:T(128)S(1)}, s32[14]{0:T(128)}, u32[]{:S(2)}) copy-start(s32[14]{0:T(128)} %reshape.6.refs_0_) | copy-start | bytes 172
  55.8 2.3 %collective-permute-start.9 = (bf16[2,128,896]{2,1,0:T(8,128)(2,1)S(1)}, bf16[2,128,896]{2,1,0:T(8,128)(2,1)S(1)}, u32[]{:S(2)}, u32[]{:S(2)}) collective-permute-start(bf16[2,128,896]{2,1,0:T(8,128)(2,1)S(1)} %get-tuple-element.29.refs_6_), channel_id=1, source_target_pairs={{0,1},{1,0},{2,3},{3,2},{4,5},{5,4},{6,7},{7,6},{8,9},{9,8},{10,11... | collective-permute-start | bytes 1376264 | tf_op jit(solution)/shard_map/ppermute | solution.py:448
  55.9 2.5 %collective-permute-start.10 = (bf16[2,128,896]{2,1,0:T(8,128)(2,1)S(1)}, bf16[2,128,896]{2,1,0:T(8,128)(2,1)S(1)}, u32[]{:S(2)}, u32[]{:S(2)}) collective-permute-start(bf16[2,128,896]{2,1,0:T(8,128)(2,1)S(1)} %get-tuple-element.30.refs_8_), channel_id=1, source_target_pairs={{0,1},{1,0},{2,3},{3,2},{4,5},{5,4},{6,7},{7,6},{8,9},{9,8},{10,11... | collective-permute-start | bytes 1376264 | tf_op jit(solution)/shard_map/ppermute | solution.py:448

commit v3 on v2

--- a/solution.py
+++ b/solution.py
@@ -18,8 +18,9 @@
 ANY = pl.BlockSpec(memory_space=pl.ANY)
 VM = pl.BlockSpec(memory_space=pltpu.VMEM)
 SM = pl.BlockSpec(memory_space=pltpu.SMEM)
-EARLY = 5
 PER = 1024
+GROUP = 4
+AHEAD = 3
 E_US, KV_US, CROSS_US = 8.0, 4.0, 6.0
 
 
@@ -97,7 +98,7 @@
     tokens = count * length
     return pl.pallas_call(
         encode_kernel,
-        out_shape=jax.ShapeDtypeStruct(rows.shape, BF),
+        out_shape=pltpu.VMEM(rows.shape, BF),
         in_specs=[VM, VM, ANY, ANY],
         out_specs=VM,
         scratch_shapes=[
@@ -107,54 +108,55 @@
             pltpu.VMEM((tokens, width), BF),
             pltpu.SemaphoreType.DMA((13,)),
         ],
-        compiler_params=pltpu.CompilerParams(vmem_limit_bytes=58 * MB),
+        compiler_params=pltpu.CompilerParams(vmem_limit_bytes=57 * MB),
         cost_estimate=cost(E_US),
         name="encode_rows",
     )(rows, gain, w_qkv, w_out)
 
 
-def gather_rows(plan, sources, ids_ref, me, rows, slots, sems, taken):
+def gather_rows(plan, sources, ids_ref, me, rows, slots, sems):
+    bottom, top, plan = plan
 
     def look(s, found):
         code = ids_ref[s]
         owner, row = lax.shift_right_logical(code, 10), jnp.bitwise_and(code, PER - 1)
-        if taken is not None:
-            taken[s] = 0
-        for source, test, place in plan(sources, owner, jnp.bitwise_xor(owner, me), row):
-
-            @pl.when(test)
-            def _():
-                slots[found] = s
-                if taken is not None:
-                    taken[s] = 1
-                pltpu.make_async_copy(source.at[place], rows.at[found], sems.at[found]).start()
-
-            found = found + test.astype(jnp.int32)
-        return found
+        hop = jnp.bitwise_xor(owner, me)
+        inside = (hop >= bottom) & (hop < top)
+
+        @pl.when(inside)
+        def _():
+            slots[found] = s
+            for source, test, place in plan(sources, owner, hop, row):
+
+                @pl.when(test)
+                def _():
+                    pltpu.make_async_copy(source.at[place], rows.at[found], sems.at[found]).start()
+
+        return found + inside.astype(jnp.int32)
 
     return lax.fori_loop(0, ids_ref.shape[0], look, jnp.int32(0))
 
 
-def project_pairs(found, source, w_ref, rows, sems, finish):
+def project_groups(found, source, w_ref, rows, sems, finish):
     length, width = rows.shape[1:]
     chunk = 1024
 
+    def arrive(i, carry):
+        pltpu.make_async_copy(source.at[0], rows.at[i], sems.at[i]).wait()
+        return carry
+
     def project(g, carry):
-        i = 2 * g
-        pltpu.make_async_copy(source.at[0], rows.at[i], sems.at[i]).wait()
-
-        @pl.when(i + 1 < found)
-        def _():
-            pltpu.make_async_copy(source.at[0], rows.at[i + 1], sems.at[i + 1]).wait()
-
-        both = rows[pl.ds(i, 2)].reshape(2 * length, width)
+        i = GROUP * g
+        lax.fori_loop(i, jnp.minimum(i + GROUP, found), arrive, 0)
+        many = rows[pl.ds(i, GROUP)].reshape(GROUP * length, width)
         for b in range(w_ref.shape[1] // chunk):
             cols = pl.ds(b * chunk, chunk)
-            out = jnp.dot(both, w_ref[:, cols], preferred_element_type=F32).astype(BF)
-            finish(i, cols, out[:length], out[length:])
+            out = jnp.dot(many, w_ref[:, cols], preferred_element_type=F32).astype(BF)
+            for j in range(GROUP):
+                finish(i + j, cols, out[j * length : (j + 1) * length])
         return carry
 
-    lax.fori_loop(0, (found + 1) // 2, project, 0)
+    lax.fori_loop(0, (found + GROUP - 1) // GROUP, project, 0)
 
 
 def kv_kernel(plan, n_src, fresh, *refs):
@@ -169,7 +171,7 @@
         ]
         for load in loads:
             load.start()
-    found = gather_rows(plan, sources, ids_ref, me_ref[0], rows, slots, sems, None)
+    found = gather_rows(plan, sources, ids_ref, me_ref[0], rows, slots, sems)
     if fresh:
         for load in loads:
             load.wait()
@@ -180,20 +182,18 @@
     def send(i, cols):
         pltpu.make_async_copy(made.at[i, :, cols], kv_hbm.at[slots[i], :, cols], out_sems.at[i]).start()
 
-    def finish(i, cols, one, two):
-        made[i, :, cols] = one
-        made[i + 1, :, cols] = two
-        send(i, cols)
-
-        @pl.when(i + 1 < found)
+    def finish(i, cols, part):
+        made[i, :, cols] = part
+
+        @pl.when(i < found)
         def _():
-            send(i + 1, cols)
+            send(i, cols)
 
     def drain(i, carry):
         store(i).wait()
         return carry
 
-    project_pairs(found, sources[0], w_ref, rows, sems, finish)
+    project_groups(found, sources[0], w_ref, rows, sems, finish)
     lax.fori_loop(0, found, drain, 0)
     token_ref[...] = jnp.zeros_like(token_ref)
 
@@ -202,8 +202,7 @@
     length, width = sources[0].shape[1:]
     features = w_kv.shape[-1]
     slots = ids.shape[0]
-    most = min(most, slots)
-    most += most % 2
+    most = -(-min(most, slots) // GROUP) * GROUP
     fresh = before is None
     operands = [ids, me, w_kv, *sources]
     specs = [SM, SM, ANY if fresh else VM] + [ANY] * len(sources)
@@ -230,7 +229,7 @@
             pltpu.SemaphoreType.DMA((8,)),
             pltpu.SemaphoreType.DMA((most,)),
         ],
-        compiler_params=pltpu.CompilerParams(vmem_limit_bytes=48 * MB),
+        compiler_params=pltpu.CompilerParams(vmem_limit_bytes=(48 if fresh else 44) * MB),
         cost_estimate=cost(KV_US),
         name="keyvals_rows",
     )(*operands)
@@ -266,63 +265,92 @@
         out_ref[here, cols] = jnp.where(first, both[:SPAN], both[SPAN:]).astype(BF)
 
 
-def final_kernel(plan, n_src, *refs):
-    ids_ref, me_ref, w_ref, kv_hbm, first_hbm, second_hbm = refs[:6]
-    sources = refs[6 : 6 + n_src]
-    out_hbm, rows, keyvals, queries, result, slots, taken, sems, kv_sems, q_sems, out_sems = refs[6 + n_src :]
-    cut = first_hbm.shape[1]
+def last_kernel(plan, n_src, *refs):
+    ids_ref, me_ref, w_ref = refs[:3]
+    sources = refs[3 : 3 + n_src]
+    made, rows, slots, sems = refs[3 + n_src :]
+    found = gather_rows(plan, sources, ids_ref, me_ref[0], rows, slots, sems)
+
+    def finish(i, cols, part):
+        made[i, :, cols] = part
+
+    project_groups(found, sources[0], w_ref, rows, sems, finish)
+
+
+def last_keyvals(ids, me, sources, w, plan):
+    length, width = sources[0].shape[1:]
+    return pl.pallas_call(
+        functools.partial(last_kernel, plan, len(sources)),
+        out_shape=pltpu.VMEM((GROUP, length, w.shape[1]), BF),
+        in_specs=[SM, SM, VM] + [ANY] * len(sources),
+        out_specs=VM,
+        scratch_shapes=[
+            pltpu.VMEM((GROUP, length, width), BF),
+            pltpu.SMEM((GROUP,), jnp.int32),
+            pltpu.SemaphoreType.DMA((GROUP,)),
+        ],
+        compiler_params=pltpu.CompilerParams(vmem_limit_bytes=40 * MB),
+        cost_estimate=cost(0.01),
+        name="last_keyvals",
+    )(ids, me, w, *sources)
+
+
+def cross_kernel(bottom, *refs):
+    ids_ref, me_ref, kv_hbm, q_hbm = refs[:4]
+    made = refs[4] if len(refs) == 12 else None
+    out_hbm, keyvals, queries, result, kv_sems, q_sems, out_sems = refs[-7:]
     tokens = queries.shape[0]
     total = ids_ref.shape[0]
     picks = total * SPAN // tokens
-    found = gather_rows(plan, sources, ids_ref, me_ref[0], rows, slots, sems, taken)
-    loads = [
-        pltpu.make_async_copy(first_hbm.at[0], queries.at[pl.ds(0, cut)], q_sems.at[0]),
-        pltpu.make_async_copy(second_hbm.at[0], queries.at[pl.ds(cut, tokens - cut)], q_sems.at[1]),
-    ]
-    for load in loads:
-        load.start()
+    spans = tokens // SPAN
+    ahead = min(AHEAD, spans)
 
     def fetch(s):
         return pltpu.make_async_copy(kv_hbm.at[s], keyvals.at[s], kv_sems.at[s])
 
-    def begin(s, carry):
-        @pl.when(taken[s] == 0)
-        def _():
-            fetch(s).start()
-
-        return carry
-
-    lax.fori_loop(0, total, begin, 0)
-
-    def finish(i, cols, one, two):
-        keyvals[slots[i], :, cols] = one
-
-        @pl.when(i + 1 < found)
-        def _():
-            keyvals[slots[i + 1], :, cols] = two
-
-    if n_src:
-        project_pairs(found, sources[0], w_ref, rows, sems, finish)
-    for load in loads:
-        load.wait()
+    def rows_of(span):
+        return pl.ds(pl.multiple_of(span * SPAN, SPAN), SPAN)
+
+    def load(span):
+        here = rows_of(span)
+        return pltpu.make_async_copy(q_hbm.at[0, here], queries.at[here], q_sems.at[span])
 
     def store(span):
-        here = pl.ds(pl.multiple_of(span * SPAN, SPAN), SPAN)
+        here = rows_of(span)
         return pltpu.make_async_copy(result.at[here], out_hbm.at[0, here], out_sems.at[span])
 
-    def attend(span, carry):
+    def begin(span, found):
+        load(span).start()
         for j in range(picks):
             s = span * picks + j
-
-            @pl.when(taken[s] == 0)
+            if made is None:
+                fetch(s).start()
+                continue
+            late = jnp.bitwise_xor(lax.shift_right_logical(ids_ref[s], 10), me_ref[0]) >= bottom
+
+            @pl.when(late)
             def _():
-                fetch(s).wait()
-
+                pltpu.make_async_copy(made.at[found], keyvals.at[s], kv_sems.at[s]).start()
+
+            @pl.when(jnp.logical_not(late))
+            def _():
+                fetch(s).start()
+
+            found = found + late.astype(jnp.int32)
+        return found
+
+    found = lax.fori_loop(0, ahead, begin, jnp.int32(0))
+
+    def attend(span, found):
+        found = lax.cond(span + ahead < spans, begin, lambda span, found: found, span + ahead, found)
+        load(span).wait()
+        for j in range(picks):
+            fetch(span * picks + j).wait()
         attend_span(span, queries, keyvals, result)
         store(span).start()
-        return carry
-
-    lax.fori_loop(0, tokens // SPAN, attend, 0)
+        return found
+
+    lax.fori_loop(0, spans, attend, found)
 
     def drain(span, carry):
         store(span).wait()
@@ -331,39 +359,34 @@
     lax.fori_loop(0, tokens // SPAN, drain, 0)
 
 
-def final(ids, me, sources, w, kv, first, second, plan, most):
-    length, width = kv.shape[1], w.shape[0]
-    slots = ids.shape[0]
-    tokens, features = first.shape[1] + second.shape[1], first.shape[2]
-    return pl.pallas_call(
-        functools.partial(final_kernel, plan, len(sources)),
+def cross(ids, me, kv, queries, made, bottom):
+    slots, length, both = kv.shape
+    tokens, features = queries.shape[1:]
+    extra = [] if made is None else [made]
+    return pl.pallas_call(
+        functools.partial(cross_kernel, bottom),
         out_shape=jax.ShapeDtypeStruct((1, tokens, features), BF),
-        in_specs=[SM, SM, VM] + [ANY] * (3 + len(sources)),
+        in_specs=[SM, SM, ANY, ANY] + [VM] * len(extra),
         out_specs=ANY,
         scratch_shapes=[
-            pltpu.VMEM((most, length, width), BF),
-            pltpu.VMEM((slots, length, kv.shape[2]), BF),
+            pltpu.VMEM((slots, length, both), BF),
             pltpu.VMEM((tokens, features), BF),
             pltpu.VMEM((tokens, features), BF),
-            pltpu.SMEM((most,), jnp.int32),
-            pltpu.SMEM((slots,), jnp.int32),
-            pltpu.SemaphoreType.DMA((most,)),
             pltpu.SemaphoreType.DMA((slots,)),
-            pltpu.SemaphoreType.DMA((2,)),
             pltpu.SemaphoreType.DMA((tokens // SPAN,)),
-        ],
-        compiler_params=pltpu.CompilerParams(vmem_limit_bytes=36 * MB),
+            pltpu.SemaphoreType.DMA((tokens // SPAN,)),
+        ],
+        compiler_params=pltpu.CompilerParams(vmem_limit_bytes=44 * MB),
         cost_estimate=cost(CROSS_US),
-        name="attend_spans",
-    )(ids, me, w, kv, first, second, *sources)
-
-
-def head_kernel(q_ref, out_ref, sems):
-    count = sems.shape[0]
-    step = out_ref.shape[1] // count
+        name="cross_spans",
+    )(ids, me, kv, queries, *extra)
+
+
+def split_kernel(x_ref, y_ref, token_ref, low_ref, high_ref, x_out, y_out, sems):
+    half = low_ref.shape[0]
     copies = [
-        pltpu.make_async_copy(q_ref.at[:, pl.ds(i * step, step)], out_ref.at[:, pl.ds(i * step, step)], sems.at[i])
-        for i in range(count)
+        pltpu.make_async_copy(x_ref.at[pl.ds(0, half)], low_ref, sems.at[0]),
+        pltpu.make_async_copy(y_ref.at[pl.ds(half, high_ref.shape[0])], high_ref, sems.at[1]),
     ]
     for copy in copies:
         copy.start()
@@ -371,54 +394,24 @@
         copy.wait()
 
 
-def head(queries, count):
-    return pl.pallas_call(
-        head_kernel,
-        out_shape=pltpu.VMEM((1, count, queries.shape[2]), BF),
-        in_specs=[ANY],
-        out_specs=VM,
-        scratch_shapes=[pltpu.SemaphoreType.DMA((count // SPAN,))],
-        compiler_params=pltpu.CompilerParams(vmem_limit_bytes=56 * MB),
-        cost_estimate=cost(1.0),
-        name="first_queries",
-    )(queries)
-
-
-def split_kernel(
-    start, x_ref, y_ref, q_ref, done_ref, token_ref, low_ref, high_ref, out_ref, x_out, y_out, sems
-):
-    half = low_ref.shape[0]
-    copies = [
-        pltpu.make_async_copy(x_ref.at[pl.ds(0, half)], low_ref, sems.at[0]),
-        pltpu.make_async_copy(y_ref.at[pl.ds(half, high_ref.shape[0])], high_ref, sems.at[1]),
-        pltpu.make_async_copy(q_ref.at[:, pl.ds(start, out_ref.shape[1])], out_ref, sems.at[2]),
-    ]
-    for copy in copies:
-        copy.start()
-    for copy in copies:
-        copy.wait()
-
-
-def split(x, y, queries, start, received, token):
-    _, tokens, width = queries.shape
+def split(x, y, token):
     half = x.shape[0] // 2
     return pl.pallas_call(
-        functools.partial(split_kernel, start),
+        split_kernel,
         out_shape=[
             pltpu.VMEM((half,) + x.shape[1:], BF),
             pltpu.VMEM((y.shape[0] - half,) + x.shape[1:], BF),
-            pltpu.VMEM((1, tokens - start, width), BF),
             jax.ShapeDtypeStruct(x.shape, BF),
             jax.ShapeDtypeStruct(y.shape, BF),
         ],
-        in_specs=[ANY, ANY, ANY, ANY, VM],
-        out_specs=[VM] * 3 + [ANY] * 2,
-        input_output_aliases={0: 3, 1: 4},
-        scratch_shapes=[pltpu.SemaphoreType.DMA((3,))],
+        in_specs=[ANY, ANY, VM],
+        out_specs=[VM] * 2 + [ANY] * 2,
+        input_output_aliases={0: 2, 1: 3},
+        scratch_shapes=[pltpu.SemaphoreType.DMA((2,))],
         compiler_params=pltpu.CompilerParams(vmem_limit_bytes=24 * MB),
-        cost_estimate=cost(1.0),
+        cost_estimate=cost(0.1),
         name="next_sends",
-    )(x, y, queries, received, token)
+    )(x, y, token)
 
 
 def relay_kernel(low_ref, high_ref, token_ref, low_out, high_out):
@@ -452,9 +445,7 @@
     dp = lax.axis_size("dp")
     slots = nb_owner.shape[1] * nb_owner.shape[2]
     per = cache_emb.shape[0]
-    spans = nb_owner.shape[1]
-    start = EARLY * spans // 7 * SPAN
-    first = shifted(head(query_states, start))
+    received = shifted(query_states)
     me = lax.axis_index("dp").astype(jnp.int32).reshape(1)
     ids = (nb_owner * PER + nb_row).reshape(-1)
     own = encode(cache_emb, enc_gain, w_qkv, w_out)
@@ -473,22 +464,21 @@
             return lows + [(src[i + 2], (hop == i + 6) & (row >= half), row - half) for i in range(2)]
 
         x, y, near = swapped(own, 2), swapped(own, 4), swapped(own, 1)
-        kv, w, token = part([own, near], w_kv, None, nearest, 4)
-        xl, yh, rest, x, y = split(x, y, query_states, start, first, token)
-        dl, dh, second = swapped(xl, 4), swapped(yh, 2), shifted(rest)
-        kv, w, token = part([x, swapped(x, 1), y, swapped(y, 1)], w, kv, middle, 8)
+        kv, w, token = part([own, near], w_kv, None, (0, 2, nearest), 4)
+        xl, yh, x, y = split(x, y, token)
+        dl, dh = swapped(xl, 4), swapped(yh, 2)
+        kv, w, token = part([x, swapped(x, 1), y, swapped(y, 1)], w, kv, (2, 6, middle), 8)
         dl, dh = relay(dl, dh, token)
-        sources = [dl, swapped(dl, 1), dh, swapped(dh, 1)]
+        made = last_keyvals(ids, me, [dl, swapped(dl, 1), dh, swapped(dh, 1)], w, (6, 8, last))
     else:
         whole = lax.all_gather(own, "dp", axis=0, tiled=True)
-        second = shifted(query_states[:, start:])
-        kv, w, _ = part([whole], w_kv, None, lambda src, owner, hop, row: [(src[0], owner >= 0, owner * per + row)], slots)
-        sources = []
-
-        def last(src, owner, hop, row):
-            return []
-
-    return final(ids, me, sources, w, kv, first, second, last, 4)
+
+        def everything(src, owner, hop, row):
+            return [(src[0], owner >= 0, owner * per + row)]
+
+        kv, w, _ = part([whole], w_kv, None, (0, 1 << 20, everything), slots)
+        made = None
+    return cross(ids, me, kv, received, made, 6)
 
 
 def solution(mesh):

time: 73.7 us -> 71.8 us (0.974); the launches traced: 72.8 us -> 71.9 us
  starting transfers between devices: 10.9 us -> 9.37 us
  waiting for transfers between devices: 12.8 us -> 11.5 us
  Pallas kernels: 47 us -> 48.2 us
    ppermute x2 -> x1, starting transfers between devices: 4.66 us -> 1.58 us  [shifted(): return lax.ppermute(block, 'section', [((i - 1) % n, i) for i in range(n)])]
    pallas_call x2, Pallas kernels: 19.6 us -> 22.1 us  [keyvals_part(): pl.pallas_call(functools.partial(kv_kernel, plan, len(sources), fresh), o...]
    ppermute x2 -> x1, waiting for transfers between devices: 1.75 us -> 0.01 us  [shifted(): return lax.ppermute(block, 'section', [((i - 1) % n, i) for i in range(n)])]
    ppermute x9, starting transfers between devices: 6.27 us -> 7.79 us  [swapped(): return lax.ppermute(block, 'dp', [(i, i ^ hop) for i in range(n)])]
    pallas_call x4, Pallas kernels: 27.4 us -> 26.1 us  [the longest x1 10.1 us: encode(): pl.pallas_call(encode_kernel, out_shape=pltpu.VMEM(rows.shape, BF), in_sp...]
    unnamed x16 -> x10, local copies, waits for them, and re-layouts: 1.24 us -> 1.86 us
  transfers between devices with their start and end apart: 11 -> 10, of which waited for: 4 -> 5; matrix products, arithmetic and copies ran while one was open for 1% -> 1% of each run, Pallas kernels for 41% -> 41%
where the time goes in v3:
time: 71.8 us; the launch traced here: 71.9 us
  Pallas kernels  48.2 us (67%)
  waiting for transfers between devices  11.5 us (16%)
  starting transfers between devices  9.37 us (13%)
  local copies, waits for them, and re-layouts  2.51 us (3%)
    pallas_call x2, Pallas kernels, keyvals_part(): pl.pallas_call(functools.partial(kv_kernel, plan, len(sources), fresh), o...  22.1 us
    ppermute x9, waiting for transfers between devices, swapped(): return lax.ppermute(block, 'dp', [(i, i ^ hop) for i in range(n)])  11.5 us
    pallas_call x1, Pallas kernels, encode(): pl.pallas_call(encode_kernel, out_shape=pltpu.VMEM(rows.shape, BF), in_sp...  10.1 us
    pallas_call x1, Pallas kernels, cross(): pl.pallas_call(functools.partial(cross_kernel, bottom), out_shape=jax.Sha...  8.71 us
    ppermute x9, starting transfers between devices, swapped(): return lax.ppermute(block, 'dp', [(i, i ^ hop) for i in range(n)])  7.79 us
    pallas_call x1, Pallas kernels, last_keyvals(): pl.pallas_call(functools.partial(last_kernel, plan, len(sources)), out_sh...  6.78 us
    unnamed x10, local copies, waits for them, and re-layouts  1.86 us
    ppermute x1, starting transfers between devices, shifted(): return lax.ppermute(block, 'section', [((i - 1) % n, i) for i in range(n)])  1.58 us
  transfers between devices with their start and end apart: 10, of which 5 were waited for; matrix products, arithmetic and copies ran while one was open for 1% of the time, Pallas kernels for 41%

profile of v3, /device:TPU:0, one launch (start us, length us, event | category | flops | bytes accessed | tf_op | source)
XLA Modules:
  0.0 71.9 jit_solution(16966893589498304443)
XLA Ops:
  0.0 0.0 copy-start.3
  0.0 0.0 copy-start.2
  0.0 10.1 %encode_rows.1.refs_3_ = bf16[4,128,896]{2,1,0:T(8,128)(2,1)} custom-call(bf16[4,128,896]{2,1,0:T(8,128)(2,1)} %rows_ref.1, f32[1,896]{1,0:T(1,128)} %gain_ref.1, bf16[1,896,2688]{2,1,0:T(8,128)(2,1)} %wqkv_hbm.1, bf16[1,896,896]{2,1,0:T(8,128)(2,1)} %wout_hbm.1), custom_call_target="tpu_custom_call" | custom-call | flops 8000000000 | bytes 1 | tf_op jit(solution)/shard_map/encode_rows/pallas_call | solution.py:99
  10.1 0.5 collective-permute-start
  10.6 2.6 %collective-permute-start.1 = (bf16[4,128,896]{2,1,0:T(8,128)(2,1)}, bf16[4,128,896]{2,1,0:T(8,128)(2,1)S(1)}, u32[]{:S(2)}, u32[]{:S(2)}) collective-permute-start(bf16[4,128,896]{2,1,0:T(8,128)(2,1)} %encode_rows.1.refs_3_), channel_id=1, source_target_pairs={{0,2},{1,3},{2,0},{3,1},{4,6},{5,7},{6,4},{7,5},{8,10},{9,11},{10,... | collective-permute-start | bytes 2752520 | tf_op jit(solution)/shard_map/ppermute | solution.py:441
  13.2 1.5 %collective-permute-start.2 = (bf16[4,128,896]{2,1,0:T(8,128)(2,1)}, bf16[4,128,896]{2,1,0:T(8,128)(2,1)S(1)}, u32[]{:S(2)}, u32[]{:S(2)}) collective-permute-start(bf16[4,128,896]{2,1,0:T(8,128)(2,1)} %encode_rows.1.refs_3_), channel_id=1, source_target_pairs={{0,4},{1,5},{2,6},{3,7},{4,0},{5,1},{6,2},{7,3},{8,12},{9,13},{10,... | collective-permute-start | bytes 2752520 | tf_op jit(solution)/shard_map/ppermute | solution.py:441
  14.7 1.6 %collective-permute-start.5 = (bf16[1,448,2048]{2,1,0:T(8,128)(2,1)}, bf16[1,448,2048]{2,1,0:T(8,128)(2,1)}, u32[]{:S(2)}, u32[]{:S(2)}) collective-permute-start(bf16[1,448,2048]{2,1,0:T(8,128)(2,1)} %param.8), channel_id=1, source_target_pairs={{24,0},{0,8},{8,16},{16,24},{25,1},{1,9},{9,17},{17,25},{26,2},{2,... | collective-permute-start | bytes 5505032 | tf_op jit(solution)/shard_map/ppermute | solution.py:436
  16.2 0.0 copy-done.3
  16.3 0.0 copy-done.2
  16.3 0.1 copy.16
  16.4 0.6 reshape.6.refs_0_
  16.9 0.0 collective-permute-done.refs_4_
  16.9 0.0 copy-start.4
  16.9 0.9 %copy-done.4 = bf16[4,128,896]{2,1,0:T(8,128)(2,1)} copy-done((bf16[4,128,896]{2,1,0:T(8,128)(2,1)}, bf16[4,128,896]{2,1,0:T(8,128)(2,1)S(1)}, u32[]{:S(2)}) %copy-start.4) | copy-done | bytes 917528
  17.8 0.0 copy-start
  17.8 9.6 %keyvals_rows.2 = (bf16[14,128,4096]{2,1,0:T(8,128)(2,1)}, bf16[896,4096]{1,0:T(8,128)(2,1)S(1)}, f32[8,128]{1,0:T(8,128)S(1)}) custom-call(s32[14]{0:T(128)} %reshape.6.refs_0_, s32[1]{0:T(128)} %bitcast.refs_1_, bf16[1,896,4096]{2,1,0:T(8,128)(2,1)} %refs_2_.1, bf16[4,128,896]{2,1,0:T(8,128)(2,1)} %encode_rows.1.refs_3_, bf16[4,128,896]{2,1,0:T(8,128)(2,1)} %copy-done.4), custom_call_target="tpu_custom_call" | custom-call | flops 4000000000 | bytes 1 | tf_op jit(solution)/shard_map/keyvals_rows/pallas_call | solution.py:214
  27.4 6.9 %collective-permute-done.1.x_ref = bf16[4,128,896]{2,1,0:T(8,128)(2,1)S(1)} collective-permute-done((bf16[4,128,896]{2,1,0:T(8,128)(2,1)}, bf16[4,128,896]{2,1,0:T(8,128)(2,1)S(1)}, u32[]{:S(2)}, u32[]{:S(2)}) %collective-permute-start.1) | collective-permute-done | bytes 917536 | tf_op jit(solution)/shard_map/ppermute | solution.py:441
  34.3 1.5 %collective-permute-done.2.y_ref = bf16[4,128,896]{2,1,0:T(8,128)(2,1)S(1)} collective-permute-done((bf16[4,128,896]{2,1,0:T(8,128)(2,1)}, bf16[4,128,896]{2,1,0:T(8,128)(2,1)S(1)}, u32[]{:S(2)}, u32[]{:S(2)}) %collective-permute-start.2) | collective-permute-done | bytes 917536 | tf_op jit(solution)/shard_map/ppermute | solution.py:441
  35.8 0.6 next_sends.1
  36.4 0.1 collective-permute-start.3
  36.4 0.5 collective-permute-start.4
  36.9 1.5 %collective-permute-start.6 = (bf16[2,128,896]{2,1,0:T(8,128)(2,1)S(1)}, bf16[2,128,896]{2,1,0:T(8,128)(2,1)S(1)}, u32[]{:S(2)}, u32[]{:S(2)}) collective-permute-start(bf16[2,128,896]{2,1,0:T(8,128)(2,1)S(1)} %get-tuple-element.24), channel_id=1, source_target_pairs={{0,4},{1,5},{2,6},{3,7},{4,0},{5,1},{6,2},{7,3},{8,12},{9,13},{10,... | collective-permute-start | bytes 1376264 | tf_op jit(solution)/shard_map/ppermute | solution.py:441
  38.4 0.5 collective-permute-start.7
  39.0 0.0 collective-permute-done.3.refs_4_
  39.0 1.2 %collective-permute-done.4.refs_6_ = bf16[4,128,896]{2,1,0:T(8,128)(2,1)S(1)} collective-permute-done((bf16[4,128,896]{2,1,0:T(8,128)(2,1)S(1)}, bf16[4,128,896]{2,1,0:T(8,128)(2,1)S(1)}, u32[]{:S(2)}, u32[]{:S(2)}) %collective-permute-start.4) | collective-permute-done | bytes 917536 | tf_op jit(solution)/shard_map/ppermute | solution.py:441
  40.2 0.0 copy-start.1
  40.2 0.9 %copy-done.1 = bf16[4,128,896]{2,1,0:T(8,128)(2,1)} copy-done((bf16[4,128,896]{2,1,0:T(8,128)(2,1)}, bf16[4,128,896]{2,1,0:T(8,128)(2,1)S(1)}, u32[]{:S(2)}) %copy-start.1) | copy-done | bytes 917528
  41.1 0.0 copy-done
  41.1 12.6 %keyvals_rows.3 = (bf16[14,128,4096]{2,1,0:T(8,128)(2,1)}, bf16[896,4096]{1,0:T(8,128)(2,1)S(1)}, f32[8,128]{1,0:T(8,128)S(1)}) custom-call(s32[14]{0:T(128)S(1)} %copy-done, s32[1]{0:T(128)} %bitcast.refs_1_, bf16[896,4096]{1,0:T(8,128)(2,1)S(1)} %get-tuple-element.17.refs_2_, ...), custom_call_target="tpu_custom_call", output_to_operand_aliasing={{1}: (2, {}), {0}: (7, {})} | custom-call | flops 4000000000 | bytes 1 | tf_op jit(solution)/shard_map/keyvals_rows/pallas_call | solution.py:214
  53.7 0.0 collective-permute-done.6.low_ref
  53.7 0.0 collective-permute-done.7.high_ref
  53.7 0.2 collective-permute-start.8
  53.9 0.4 collective-permute-start.9
  54.3 1.3 %collective-permute-done.8.refs_4_ = bf16[2,128,896]{2,1,0:T(8,128)(2,1)S(1)} collective-permute-done((bf16[2,128,896]{2,1,0:T(8,128)(2,1)S(1)}, bf16[2,128,896]{2,1,0:T(8,128)(2,1)S(1)}, u32[]{:S(2)}, u32[]{:S(2)}) %collective-permute-start.8) | collective-permute-done | bytes 458784 | tf_op jit(solution)/shard_map/ppermute | solution.py:441
  55.6 0.7 collective-permute-done.9.refs_6_
  56.3 6.8 %last_keyvals.1.refs_4_ = bf16[4,128,4096]{2,1,0:T(8,128)(2,1)S(1)} custom-call(s32[14]{0:T(128)S(1)} %copy-done, s32[1]{0:T(128)} %bitcast.refs_1_, bf16[896,4096]{1,0:T(8,128)(2,1)S(1)} %get-tuple-element.23.refs_2_, bf16[2,128,896]{2,1,0:T(8,128)(2,1)S(1)} %get-tuple-element.27.refs_3_, bf16[2,128,896]{2,1,0:T(8,128)(2,1)S(1)} %collective-permute-done.8.refs_4_, ...), custom_call_target="tpu_custom_call" | custom-call | flops 10000000 | bytes 1 | tf_op jit(solution)/shard_map/last_keyvals/pallas_call | solution.py:282
  63.0 0.0 collective-permute-done.5.refs_3_
  63.1 8.7 %cross_spans.1 = bf16[1,448,2048]{2,1,0:T(8,128)(2,1)} custom-call(s32[14]{0:T(128)S(1)} %copy-done, s32[1]{0:T(128)} %bitcast.refs_1_, bf16[14,128,4096]{2,1,0:T(8,128)(2,1)} %get-tuple-element.22.refs_2_, bf16[1,448,2048]{2,1,0:T(8,128)(2,1)} %collective-permute-done.5.refs_3_, bf16[4,128,4096]{2,1,0:T(8,128)(2,1)S(1)} %last_keyvals.1.refs_4_), custom_call_target="tpu_custom_call" | custom-call | flops 6000000000 | bytes 1 | tf_op jit(solution)/shard_map/cross_spans/pallas_call | solution.py:366
  (2 shorter events, 0.0 us)
Async XLA Ops:
  0.0 16.3 %copy-start.3 = (s32[1,7,2]{1,2,0:T(2,128)S(1)}, s32[1,7,2]{1,2,0:T(2,128)}, u32[]{:S(2)}) copy-start(s32[1,7,2]{1,2,0:T(2,128)} %param.10) | copy-start | bytes 172
  0.0 16.3 %copy-start.2 = (s32[1,7,2]{1,2,0:T(2,128)S(1)}, s32[1,7,2]{1,2,0:T(2,128)}, u32[]{:S(2)}) copy-start(s32[1,7,2]{1,2,0:T(2,128)} %param.11) | copy-start | bytes 172
  10.1 6.9 %collective-permute-start = (bf16[4,128,896]{2,1,0:T(8,128)(2,1)}, bf16[4,128,896]{2,1,0:T(8,128)(2,1)S(1)}, u32[]{:S(2)}, u32[]{:S(2)}) collective-permute-start(bf16[4,128,896]{2,1,0:T(8,128)(2,1)} %encode_rows.1.refs_3_), channel_id=1, source_target_pairs={{0,1},{1,0},{2,3},{3,2},{4,5},{5,4},{6,7},{7,6},{8,9},{9,8},{10,11... | collective-permute-start | bytes 2752520 | tf_op jit(solution)/shard_map/ppermute | solution.py:441
  10.6 23.7 %collective-permute-start.1 = (bf16[4,128,896]{2,1,0:T(8,128)(2,1)}, bf16[4,128,896]{2,1,0:T(8,128)(2,1)S(1)}, u32[]{:S(2)}, u32[]{:S(2)}) collective-permute-start(bf16[4,128,896]{2,1,0:T(8,128)(2,1)} %encode_rows.1.refs_3_), channel_id=1, source_target_pairs={{0,2},{1,3},{2,0},{3,1},{4,6},{5,7},{6,4},{7,5},{8,10},{9,11},{10,... | collective-permute-start | bytes 2752520 | tf_op jit(solution)/shard_map/ppermute | solution.py:441
  13.2 22.6 %collective-permute-start.2 = (bf16[4,128,896]{2,1,0:T(8,128)(2,1)}, bf16[4,128,896]{2,1,0:T(8,128)(2,1)S(1)}, u32[]{:S(2)}, u32[]{:S(2)}) collective-permute-start(bf16[4,128,896]{2,1,0:T(8,128)(2,1)} %encode_rows.1.refs_3_), channel_id=1, source_target_pairs={{0,4},{1,5},{2,6},{3,7},{4,0},{5,1},{6,2},{7,3},{8,12},{9,13},{10,... | collective-permute-start | bytes 2752520 | tf_op jit(solution)/shard_map/ppermute | solution.py:441
  14.7 48.4 %collective-permute-start.5 = (bf16[1,448,2048]{2,1,0:T(8,128)(2,1)}, bf16[1,448,2048]{2,1,0:T(8,128)(2,1)}, u32[]{:S(2)}, u32[]{:S(2)}) collective-permute-start(bf16[1,448,2048]{2,1,0:T(8,128)(2,1)} %param.8), channel_id=1, source_target_pairs={{24,0},{0,8},{8,16},{16,24},{25,1},{1,9},{9,17},{17,25},{26,2},{2,... | collective-permute-start | bytes 5505032 | tf_op jit(solution)/shard_map/ppermute | solution.py:436
  16.9 0.9 %copy-start.4 = (bf16[4,128,896]{2,1,0:T(8,128)(2,1)}, bf16[4,128,896]{2,1,0:T(8,128)(2,1)S(1)}, u32[]{:S(2)}) copy-start(bf16[4,128,896]{2,1,0:T(8,128)(2,1)S(1)} %collective-permute-done.refs_4_) | copy-start | bytes 2752516
  17.8 23.3 %copy-start = (s32[14]{0:T(128)S(1)}, s32[14]{0:T(128)}, u32[]{:S(2)}) copy-start(s32[14]{0:T(128)} %reshape.6.refs_0_) | copy-start | bytes 172
  36.4 2.6 %collective-permute-start.3 = (bf16[4,128,896]{2,1,0:T(8,128)(2,1)S(1)}, bf16[4,128,896]{2,1,0:T(8,128)(2,1)S(1)}, u32[]{:S(2)}, u32[]{:S(2)}) collective-permute-start(bf16[4,128,896]{2,1,0:T(8,128)(2,1)S(1)} %get-tuple-element.19.refs_3_), channel_id=1, source_target_pairs={{0,1},{1,0},{2,3},{3,2},{4,5},{5,4},{6,7},{7,6},{8,9},{9,8},{10,11... | collective-permute-start | bytes 2752520 | tf_op jit(solution)/shard_map/ppermute | solution.py:441
  36.4 3.8 %collective-permute-start.4 = (bf16[4,128,896]{2,1,0:T(8,128)(2,1)S(1)}, bf16[4,128,896]{2,1,0:T(8,128)(2,1)S(1)}, u32[]{:S(2)}, u32[]{:S(2)}) collective-permute-start(bf16[4,128,896]{2,1,0:T(8,128)(2,1)S(1)} %get-tuple-element.20.refs_5_), channel_id=1, source_target_pairs={{0,1},{1,0},{2,3},{3,2},{4,5},{5,4},{6,7},{7,6},{8,9},{9,8},{10,11... | collective-permute-start | bytes 2752520 | tf_op jit(solution)/shard_map/ppermute | solution.py:441
  36.9 16.8 %collective-permute-start.6 = (bf16[2,128,896]{2,1,0:T(8,128)(2,1)S(1)}, bf16[2,128,896]{2,1,0:T(8,128)(2,1)S(1)}, u32[]{:S(2)}, u32[]{:S(2)}) collective-permute-start(bf16[2,128,896]{2,1,0:T(8,128)(2,1)S(1)} %get-tuple-element.24), channel_id=1, source_target_pairs={{0,4},{1,5},{2,6},{3,7},{4,0},{5,1},{6,2},{7,3},{8,12},{9,13},{10,... | collective-permute-start | bytes 1376264 | tf_op jit(solution)/shard_map/ppermute | solution.py:441
  38.4 15.3 %collective-permute-start.7 = (bf16[2,128,896]{2,1,0:T(8,128)(2,1)S(1)}, bf16[2,128,896]{2,1,0:T(8,128)(2,1)S(1)}, u32[]{:S(2)}, u32[]{:S(2)}) collective-permute-start(bf16[2,128,896]{2,1,0:T(8,128)(2,1)S(1)} %get-tuple-element.25), channel_id=1, source_target_pairs={{0,2},{1,3},{2,0},{3,1},{4,6},{5,7},{6,4},{7,5},{8,10},{9,11},{10,... | collective-permute-start | bytes 1376264 | tf_op jit(solution)/shard_map/ppermute | solution.py:441
  40.2 0.9 %copy-start.1 = (bf16[4,128,896]{2,1,0:T(8,128)(2,1)}, bf16[4,128,896]{2,1,0:T(8,128)(2,1)S(1)}, u32[]{:S(2)}) copy-start(bf16[4,128,896]{2,1,0:T(8,128)(2,1)S(1)} %collective-permute-done.4.refs_6_) | copy-start | bytes 2752516
  53.7 1.9 %collective-permute-start.8 = (bf16[2,128,896]{2,1,0:T(8,128)(2,1)S(1)}, bf16[2,128,896]{2,1,0:T(8,128)(2,1)S(1)}, u32[]{:S(2)}, u32[]{:S(2)}) collective-permute-start(bf16[2,128,896]{2,1,0:T(8,128)(2,1)S(1)} %get-tuple-element.27.refs_3_), channel_id=1, source_target_pairs={{0,1},{1,0},{2,3},{3,2},{4,5},{5,4},{6,7},{7,6},{8,9},{9,8},{10,11... | collective-permute-start | bytes 1376264 | tf_op jit(solution)/shard_map/ppermute | solution.py:441
  53.9 2.4 %collective-permute-start.9 = (bf16[2,128,896]{2,1,0:T(8,128)(2,1)S(1)}, bf16[2,128,896]{2,1,0:T(8,128)(2,1)S(1)}, u32[]{:S(2)}, u32[]{:S(2)}) collective-permute-start(bf16[2,128,896]{2,1,0:T(8,128)(2,1)S(1)} %get-tuple-element.28.refs_5_), channel_id=1, source_target_pairs={{0,1},{1,0},{2,3},{3,2},{4,5},{5,4},{6,7},{7,6},{8,9},{9,8},{10,11... | collective-permute-start | bytes 1376264 | tf_op jit(solution)/shard_map/ppermute | solution.py:441

commit v4 on v3

--- a/solution.py
+++ b/solution.py
@@ -229,7 +229,7 @@
             pltpu.SemaphoreType.DMA((8,)),
             pltpu.SemaphoreType.DMA((most,)),
         ],
-        compiler_params=pltpu.CompilerParams(vmem_limit_bytes=(48 if fresh else 44) * MB),
+        compiler_params=pltpu.CompilerParams(vmem_limit_bytes=(46 if fresh else 42) * MB),
         cost_estimate=cost(KV_US),
         name="keyvals_rows",
     )(*operands)

time: 71.8 us -> 70.3 us (0.979)
  local copies, waits for them, and re-layouts: 2.51 us -> 0.18 us
  waiting for transfers between devices: 11.5 us -> 12.8 us
  Pallas kernels: 48.2 us -> 47.4 us
    unnamed x10 -> x4, local copies, waits for them, and re-layouts: 1.86 us -> 0.01 us
    ppermute x9, waiting for transfers between devices: 11.5 us -> 12.8 us  [swapped(): return lax.ppermute(block, 'dp', [(i, i ^ hop) for i in range(n)])]
    pallas_call x1, Pallas kernels: 10.1 us -> 9.13 us  [encode(): pl.pallas_call(encode_kernel, out_shape=pltpu.VMEM(rows.shape, BF), in_sp...]
  transfers between devices with their start and end apart: 10 -> 10, of which waited for: 5 -> 5; matrix products, arithmetic and copies ran while one was open for 1% -> 0% of each run, Pallas kernels for 41% -> 43%
where the time goes in v4:
time: 70.3 us; the launch traced here: 70.1 us
  Pallas kernels  47.4 us (67%)
  waiting for transfers between devices  12.8 us (18%)
  starting transfers between devices  9.38 us (13%)
    pallas_call x2, Pallas kernels, keyvals_part(): pl.pallas_call(functools.partial(kv_kernel, plan, len(sources), fresh), o...  22.7 us
    ppermute x9, waiting for transfers between devices, swapped(): return lax.ppermute(block, 'dp', [(i, i ^ hop) for i in range(n)])  12.8 us
    pallas_call x1, Pallas kernels, encode(): pl.pallas_call(encode_kernel, out_shape=pltpu.VMEM(rows.shape, BF), in_sp...  9.13 us
    pallas_call x1, Pallas kernels, cross(): pl.pallas_call(functools.partial(cross_kernel, bottom), out_shape=jax.Sha...  8.25 us
    ppermute x9, starting transfers between devices, swapped(): return lax.ppermute(block, 'dp', [(i, i ^ hop) for i in range(n)])  7.8 us
    pallas_call x1, Pallas kernels, last_keyvals(): pl.pallas_call(functools.partial(last_kernel, plan, len(sources)), out_sh...  6.78 us
    ppermute x1, starting transfers between devices, shifted(): return lax.ppermute(block, 'section', [((i - 1) % n, i) for i in range(n)])  1.58 us
  transfers between devices with their start and end apart: 10, of which 5 were waited for; matrix products, arithmetic and copies ran while one was open for 0% of the time, Pallas kernels for 43%

profile of v4, /device:TPU:0, one launch (start us, length us, event | category | flops | bytes accessed | tf_op | source)
XLA Modules:
  0.0 70.1 jit_solution(16309099872149854728)
XLA Ops:
  0.0 0.0 copy-start.1
  0.0 0.0 copy-start
  0.0 9.1 %encode_rows.1.refs_3_ = bf16[4,128,896]{2,1,0:T(8,128)(2,1)S(1)} custom-call(bf16[4,128,896]{2,1,0:T(8,128)(2,1)} %rows_ref.1, f32[1,896]{1,0:T(1,128)} %gain_ref.1, bf16[1,896,2688]{2,1,0:T(8,128)(2,1)} %wqkv_hbm.1, bf16[1,896,896]{2,1,0:T(8,128)(2,1)} %wout_hbm.1), custom_call_target="tpu_custom_call" | custom-call | flops 8000000000 | bytes 1 | tf_op jit(solution)/shard_map/encode_rows/pallas_call | solution.py:99
  9.1 0.5 collective-permute-start
  9.7 2.6 %collective-permute-start.1 = (bf16[4,128,896]{2,1,0:T(8,128)(2,1)S(1)}, bf16[4,128,896]{2,1,0:T(8,128)(2,1)S(1)}, u32[]{:S(2)}, u32[]{:S(2)}) collective-permute-start(bf16[4,128,896]{2,1,0:T(8,128)(2,1)S(1)} %encode_rows.1.refs_3_), channel_id=1, source_target_pairs={{0,2},{1,3},{2,0},{3,1},{4,6},{5,7},{6,4},{7,5},{8,10},{9,11},{10,... | collective-permute-start | bytes 2752520 | tf_op jit(solution)/shard_map/ppermute | solution.py:441
  12.2 1.5 %collective-permute-start.2 = (bf16[4,128,896]{2,1,0:T(8,128)(2,1)S(1)}, bf16[4,128,896]{2,1,0:T(8,128)(2,1)S(1)}, u32[]{:S(2)}, u32[]{:S(2)}) collective-permute-start(bf16[4,128,896]{2,1,0:T(8,128)(2,1)S(1)} %encode_rows.1.refs_3_), channel_id=1, source_target_pairs={{0,4},{1,5},{2,6},{3,7},{4,0},{5,1},{6,2},{7,3},{8,12},{9,13},{10,... | collective-permute-start | bytes 2752520 | tf_op jit(solution)/shard_map/ppermute | solution.py:441
  13.7 1.6 %collective-permute-start.5 = (bf16[1,448,2048]{2,1,0:T(8,128)(2,1)}, bf16[1,448,2048]{2,1,0:T(8,128)(2,1)}, u32[]{:S(2)}, u32[]{:S(2)}) collective-permute-start(bf16[1,448,2048]{2,1,0:T(8,128)(2,1)} %param.8), channel_id=1, source_target_pairs={{24,0},{0,8},{8,16},{16,24},{25,1},{1,9},{9,17},{17,25},{26,2},{2,... | collective-permute-start | bytes 5505032 | tf_op jit(solution)/shard_map/ppermute | solution.py:436
  15.3 0.0 copy-done.1
  15.3 0.0 copy-done
  15.3 0.1 copy.16
  15.4 0.1 reshape.6.refs_0_
  15.5 0.0 collective-permute-done.refs_4_
  15.5 9.5 %keyvals_rows.2 = (bf16[14,128,4096]{2,1,0:T(8,128)(2,1)}, bf16[896,4096]{1,0:T(8,128)(2,1)S(1)}, f32[8,128]{1,0:T(8,128)S(1)}) custom-call(s32[14]{0:T(128)S(1)} %reshape.6.refs_0_, s32[1]{0:T(128)} %bitcast.refs_1_, bf16[1,896,4096]{2,1,0:T(8,128)(2,1)} %refs_2_.1, bf16[4,128,896]{2,1,0:T(8,128)(2,1)S(1)} %encode_rows.1.refs_3_, ...), custom_call_target="tpu_custom_call" | custom-call | flops 4000000000 | bytes 1 | tf_op jit(solution)/shard_map/keyvals_rows/pallas_call | solution.py:214
  25.0 8.2 %collective-permute-done.1.x_ref = bf16[4,128,896]{2,1,0:T(8,128)(2,1)S(1)} collective-permute-done((bf16[4,128,896]{2,1,0:T(8,128)(2,1)S(1)}, bf16[4,128,896]{2,1,0:T(8,128)(2,1)S(1)}, u32[]{:S(2)}, u32[]{:S(2)}) %collective-permute-start.1) | collective-permute-done | bytes 917536 | tf_op jit(solution)/shard_map/ppermute | solution.py:441
  33.2 1.5 %collective-permute-done.2.y_ref = bf16[4,128,896]{2,1,0:T(8,128)(2,1)S(1)} collective-permute-done((bf16[4,128,896]{2,1,0:T(8,128)(2,1)S(1)}, bf16[4,128,896]{2,1,0:T(8,128)(2,1)S(1)}, u32[]{:S(2)}, u32[]{:S(2)}) %collective-permute-start.2) | collective-permute-done | bytes 917536 | tf_op jit(solution)/shard_map/ppermute | solution.py:441
  34.7 0.6 next_sends.1
  35.2 0.1 collective-permute-start.3
  35.3 0.5 collective-permute-start.4
  35.8 1.5 %collective-permute-start.6 = (bf16[2,128,896]{2,1,0:T(8,128)(2,1)S(1)}, bf16[2,128,896]{2,1,0:T(8,128)(2,1)S(1)}, u32[]{:S(2)}, u32[]{:S(2)}) collective-permute-start(bf16[2,128,896]{2,1,0:T(8,128)(2,1)S(1)} %get-tuple-element.24), channel_id=1, source_target_pairs={{0,4},{1,5},{2,6},{3,7},{4,0},{5,1},{6,2},{7,3},{8,12},{9,13},{10,... | collective-permute-start | bytes 1376264 | tf_op jit(solution)/shard_map/ppermute | solution.py:441
  37.3 0.5 collective-permute-start.7
  37.8 0.0 collective-permute-done.3.refs_4_
  37.9 1.2 %collective-permute-done.4.refs_6_ = bf16[4,128,896]{2,1,0:T(8,128)(2,1)S(1)} collective-permute-done((bf16[4,128,896]{2,1,0:T(8,128)(2,1)S(1)}, bf16[4,128,896]{2,1,0:T(8,128)(2,1)S(1)}, u32[]{:S(2)}, u32[]{:S(2)}) %collective-permute-start.4) | collective-permute-done | bytes 917536 | tf_op jit(solution)/shard_map/ppermute | solution.py:441
  39.1 13.2 %keyvals_rows.3 = (bf16[14,128,4096]{2,1,0:T(8,128)(2,1)}, bf16[896,4096]{1,0:T(8,128)(2,1)S(1)}, f32[8,128]{1,0:T(8,128)S(1)}) custom-call(s32[14]{0:T(128)S(1)} %reshape.6.refs_0_, s32[1]{0:T(128)} %bitcast.refs_1_, bf16[896,4096]{1,0:T(8,128)(2,1)S(1)} %get-tuple-element.17.refs_2_, ...), custom_call_target="tpu_custom_call", output_to_operand_aliasing={{1}: (2, {}), {0}: (7, {})} | custom-call | flops 4000000000 | bytes 1 | tf_op jit(solution)/shard_map/keyvals_rows/pallas_call | solution.py:214
  52.3 0.0 collective-permute-done.6.low_ref
  52.3 0.0 collective-permute-done.7.high_ref
  52.3 0.3 collective-permute-start.8
  52.6 0.3 collective-permute-start.9
  52.9 1.3 %collective-permute-done.8.refs_4_ = bf16[2,128,896]{2,1,0:T(8,128)(2,1)S(1)} collective-permute-done((bf16[2,128,896]{2,1,0:T(8,128)(2,1)S(1)}, bf16[2,128,896]{2,1,0:T(8,128)(2,1)S(1)}, u32[]{:S(2)}, u32[]{:S(2)}) %collective-permute-start.8) | collective-permute-done | bytes 458784 | tf_op jit(solution)/shard_map/ppermute | solution.py:441
  54.2 0.7 collective-permute-done.9.refs_6_
  54.9 6.8 %last_keyvals.1.refs_4_ = bf16[4,128,4096]{2,1,0:T(8,128)(2,1)S(1)} custom-call(s32[14]{0:T(128)S(1)} %reshape.6.refs_0_, s32[1]{0:T(128)} %bitcast.refs_1_, bf16[896,4096]{1,0:T(8,128)(2,1)S(1)} %get-tuple-element.23.refs_2_, bf16[2,128,896]{2,1,0:T(8,128)(2,1)S(1)} %get-tuple-element.27.refs_3_, bf16[2,128,896]{2,1,0:T(8,128)(2,1)S(1)} %collective-permute-done.8.refs_4_, ...), custom_call_target="tpu_custom_call" | custom-call | flops 10000000 | bytes 1 | tf_op jit(solution)/shard_map/last_keyvals/pallas_call | solution.py:282
  61.7 0.0 collective-permute-done.5.refs_3_
  61.7 8.3 %cross_spans.1 = bf16[1,448,2048]{2,1,0:T(8,128)(2,1)} custom-call(s32[14]{0:T(128)S(1)} %reshape.6.refs_0_, s32[1]{0:T(128)} %bitcast.refs_1_, bf16[14,128,4096]{2,1,0:T(8,128)(2,1)} %get-tuple-element.22.refs_2_, bf16[1,448,2048]{2,1,0:T(8,128)(2,1)} %collective-permute-done.5.refs_3_, bf16[4,128,4096]{2,1,0:T(8,128)(2,1)S(1)} %last_keyvals.1.refs_4_), custom_call_target="tpu_custom_call" | custom-call | flops 6000000000 | bytes 1 | tf_op jit(solution)/shard_map/cross_spans/pallas_call | solution.py:366
  (2 shorter events, 0.0 us)
Async XLA Ops:
  0.0 15.3 %copy-start.1 = (s32[1,7,2]{1,2,0:T(2,128)S(1)}, s32[1,7,2]{1,2,0:T(2,128)}, u32[]{:S(2)}) copy-start(s32[1,7,2]{1,2,0:T(2,128)} %param.10) | copy-start | bytes 172
  0.0 15.3 %copy-start = (s32[1,7,2]{1,2,0:T(2,128)S(1)}, s32[1,7,2]{1,2,0:T(2,128)}, u32[]{:S(2)}) copy-start(s32[1,7,2]{1,2,0:T(2,128)} %param.11) | copy-start | bytes 172
  9.1 6.4 %collective-permute-start = (bf16[4,128,896]{2,1,0:T(8,128)(2,1)S(1)}, bf16[4,128,896]{2,1,0:T(8,128)(2,1)}, u32[]{:S(2)}, u32[]{:S(2)}) collective-permute-start(bf16[4,128,896]{2,1,0:T(8,128)(2,1)S(1)} %encode_rows.1.refs_3_), channel_id=1, source_target_pairs={{0,1},{1,0},{2,3},{3,2},{4,5},{5,4},{6,7},{7,6},{8,9},{9,8},{10,11... | collective-permute-start | bytes 2752520 | tf_op jit(solution)/shard_map/ppermute | solution.py:441
  9.7 23.5 %collective-permute-start.1 = (bf16[4,128,896]{2,1,0:T(8,128)(2,1)S(1)}, bf16[4,128,896]{2,1,0:T(8,128)(2,1)S(1)}, u32[]{:S(2)}, u32[]{:S(2)}) collective-permute-start(bf16[4,128,896]{2,1,0:T(8,128)(2,1)S(1)} %encode_rows.1.refs_3_), channel_id=1, source_target_pairs={{0,2},{1,3},{2,0},{3,1},{4,6},{5,7},{6,4},{7,5},{8,10},{9,11},{10,... | collective-permute-start | bytes 2752520 | tf_op jit(solution)/shard_map/ppermute | solution.py:441
  12.2 22.4 %collective-permute-start.2 = (bf16[4,128,896]{2,1,0:T(8,128)(2,1)S(1)}, bf16[4,128,896]{2,1,0:T(8,128)(2,1)S(1)}, u32[]{:S(2)}, u32[]{:S(2)}) collective-permute-start(bf16[4,128,896]{2,1,0:T(8,128)(2,1)S(1)} %encode_rows.1.refs_3_), channel_id=1, source_target_pairs={{0,4},{1,5},{2,6},{3,7},{4,0},{5,1},{6,2},{7,3},{8,12},{9,13},{10,... | collective-permute-start | bytes 2752520 | tf_op jit(solution)/shard_map/ppermute | solution.py:441
  13.7 47.9 %collective-permute-start.5 = (bf16[1,448,2048]{2,1,0:T(8,128)(2,1)}, bf16[1,448,2048]{2,1,0:T(8,128)(2,1)}, u32[]{:S(2)}, u32[]{:S(2)}) collective-permute-start(bf16[1,448,2048]{2,1,0:T(8,128)(2,1)} %param.8), channel_id=1, source_target_pairs={{24,0},{0,8},{8,16},{16,24},{25,1},{1,9},{9,17},{17,25},{26,2},{2,... | collective-permute-start | bytes 5505032 | tf_op jit(solution)/shard_map/ppermute | solution.py:436
  35.2 2.6 %collective-permute-start.3 = (bf16[4,128,896]{2,1,0:T(8,128)(2,1)S(1)}, bf16[4,128,896]{2,1,0:T(8,128)(2,1)S(1)}, u32[]{:S(2)}, u32[]{:S(2)}) collective-permute-start(bf16[4,128,896]{2,1,0:T(8,128)(2,1)S(1)} %get-tuple-element.19.refs_3_), channel_id=1, source_target_pairs={{0,1},{1,0},{2,3},{3,2},{4,5},{5,4},{6,7},{7,6},{8,9},{9,8},{10,11... | collective-permute-start | bytes 2752520 | tf_op jit(solution)/shard_map/ppermute | solution.py:441
  35.3 3.8 %collective-permute-start.4 = (bf16[4,128,896]{2,1,0:T(8,128)(2,1)S(1)}, bf16[4,128,896]{2,1,0:T(8,128)(2,1)S(1)}, u32[]{:S(2)}, u32[]{:S(2)}) collective-permute-start(bf16[4,128,896]{2,1,0:T(8,128)(2,1)S(1)} %get-tuple-element.20.refs_5_), channel_id=1, source_target_pairs={{0,1},{1,0},{2,3},{3,2},{4,5},{5,4},{6,7},{7,6},{8,9},{9,8},{10,11... | collective-permute-start | bytes 2752520 | tf_op jit(solution)/shard_map/ppermute | solution.py:441
  35.8 16.5 %collective-permute-start.6 = (bf16[2,128,896]{2,1,0:T(8,128)(2,1)S(1)}, bf16[2,128,896]{2,1,0:T(8,128)(2,1)S(1)}, u32[]{:S(2)}, u32[]{:S(2)}) collective-permute-start(bf16[2,128,896]{2,1,0:T(8,128)(2,1)S(1)} %get-tuple-element.24), channel_id=1, source_target_pairs={{0,4},{1,5},{2,6},{3,7},{4,0},{5,1},{6,2},{7,3},{8,12},{9,13},{10,... | collective-permute-start | bytes 1376264 | tf_op jit(solution)/shard_map/ppermute | solution.py:441
  37.3 15.0 %collective-permute-start.7 = (bf16[2,128,896]{2,1,0:T(8,128)(2,1)S(1)}, bf16[2,128,896]{2,1,0:T(8,128)(2,1)S(1)}, u32[]{:S(2)}, u32[]{:S(2)}) collective-permute-start(bf16[2,128,896]{2,1,0:T(8,128)(2,1)S(1)} %get-tuple-element.25), channel_id=1, source_target_pairs={{0,2},{1,3},{2,0},{3,1},{4,6},{5,7},{6,4},{7,5},{8,10},{9,11},{10,... | collective-permute-start | bytes 1376264 | tf_op jit(solution)/shard_map/ppermute | solution.py:441
  52.3 1.9 %collective-permute-start.8 = (bf16[2,128,896]{2,1,0:T(8,128)(2,1)S(1)}, bf16[2,128,896]{2,1,0:T(8,128)(2,1)S(1)}, u32[]{:S(2)}, u32[]{:S(2)}) collective-permute-start(bf16[2,128,896]{2,1,0:T(8,128)(2,1)S(1)} %get-tuple-element.27.refs_3_), channel_id=1, source_target_pairs={{0,1},{1,0},{2,3},{3,2},{4,5},{5,4},{6,7},{7,6},{8,9},{9,8},{10,11... | collective-permute-start | bytes 1376264 | tf_op jit(solution)/shard_map/ppermute | solution.py:441
  52.6 2.3 %collective-permute-start.9 = (bf16[2,128,896]{2,1,0:T(8,128)(2,1)S(1)}, bf16[2,128,896]{2,1,0:T(8,128)(2,1)S(1)}, u32[]{:S(2)}, u32[]{:S(2)}) collective-permute-start(bf16[2,128,896]{2,1,0:T(8,128)(2,1)S(1)} %get-tuple-element.28.refs_5_), channel_id=1, source_target_pairs={{0,1},{1,0},{2,3},{3,2},{4,5},{5,4},{6,7},{7,6},{8,9},{9,8},{10,11... | collective-permute-start | bytes 1376264 | tf_op jit(solution)/shard_map/ppermute | solution.py:441

commit v5 on v4

--- a/solution.py
+++ b/solution.py
@@ -20,7 +20,7 @@
 SM = pl.BlockSpec(memory_space=pltpu.SMEM)
 PER = 1024
 GROUP = 4
-AHEAD = 3
+AHEAD = 4
 E_US, KV_US, CROSS_US = 8.0, 4.0, 6.0
 
 
@@ -29,9 +29,11 @@
 
 
 def encode_kernel(
-    rows_ref, gain_ref, wqkv_hbm, wout_hbm, out_ref, wqkv, wout, proj, ctx, sems
+    rows_hbm, gain_ref, wqkv_hbm, wout_hbm, out_ref, rows_ref, wqkv, wout, proj, ctx, sems
 ):
     count, length, width = rows_ref.shape
+    load = pltpu.make_async_copy(rows_hbm, rows_ref, sems.at[13])
+    load.start()
     step = width // 4
     pieces = [
         [
@@ -49,6 +51,7 @@
         for copy in piece:
             copy.start()
     last.start()
+    load.wait()
     tokens = rows_ref[...].reshape(count * length, width)
     floats = tokens.astype(F32)
     factor = lax.rsqrt(jnp.mean(floats * floats, axis=-1, keepdims=True) + 1e-06)
@@ -99,14 +102,15 @@
     return pl.pallas_call(
         encode_kernel,
         out_shape=pltpu.VMEM(rows.shape, BF),
-        in_specs=[VM, VM, ANY, ANY],
+        in_specs=[ANY, VM, ANY, ANY],
         out_specs=VM,
         scratch_shapes=[
+            pltpu.VMEM(rows.shape, BF),
             pltpu.VMEM((width, 3 * width), BF),
             pltpu.VMEM((width, width), BF),
             pltpu.VMEM((tokens, 3 * width), BF),
             pltpu.VMEM((tokens, width), BF),
-            pltpu.SemaphoreType.DMA((13,)),
+            pltpu.SemaphoreType.DMA((14,)),
         ],
         compiler_params=pltpu.CompilerParams(vmem_limit_bytes=57 * MB),
         cost_estimate=cost(E_US),

time: 70.3 us -> 70 us (level)
  no operation moved by 1% of the time
where the time goes in v5:
time: 70 us
  Pallas kernels  47.3 us (68%)
  waiting for transfers between devices  12.9 us (18%)
  starting transfers between devices  9.38 us (13%)
    pallas_call x2, Pallas kernels, keyvals_part(): pl.pallas_call(functools.partial(kv_kernel, plan, len(sources), fresh), o...  22.7 us
    ppermute x9, waiting for transfers between devices, swapped(): return lax.ppermute(block, 'dp', [(i, i ^ hop) for i in range(n)])  12.9 us
    pallas_call x1, Pallas kernels, encode(): pl.pallas_call(encode_kernel, out_shape=pltpu.VMEM(rows.shape, BF), in_sp...  8.92 us
    pallas_call x1, Pallas kernels, cross(): pl.pallas_call(functools.partial(cross_kernel, bottom), out_shape=jax.Sha...  8.62 us
    ppermute x9, starting transfers between devices, swapped(): return lax.ppermute(block, 'dp', [(i, i ^ hop) for i in range(n)])  7.8 us
    pallas_call x1, Pallas kernels, last_keyvals(): pl.pallas_call(functools.partial(last_kernel, plan, len(sources)), out_sh...  6.47 us
    ppermute x1, starting transfers between devices, shifted(): return lax.ppermute(block, 'section', [((i - 1) % n, i) for i in range(n)])  1.58 us
  transfers between devices with their start and end apart: 10, of which 5 were waited for; matrix products, arithmetic and copies ran while one was open for 0% of the time, Pallas kernels for 43%

profile of v5, /device:TPU:0, one launch (start us, length us, event | category | flops | bytes accessed | tf_op | source)
XLA Modules:
  0.0 70.0 jit_solution(4516257832208877847)
XLA Ops:
  0.0 0.0 copy-start.1
  0.0 0.0 copy-start
  0.0 8.9 %encode_rows.1.refs_3_ = bf16[4,128,896]{2,1,0:T(8,128)(2,1)S(1)} custom-call(bf16[4,128,896]{2,1,0:T(8,128)(2,1)} %rows_hbm.1, f32[1,896]{1,0:T(1,128)} %gain_ref.1, bf16[1,896,2688]{2,1,0:T(8,128)(2,1)} %wqkv_hbm.1, bf16[1,896,896]{2,1,0:T(8,128)(2,1)} %wout_hbm.1), custom_call_target="tpu_custom_call" | custom-call | flops 8000000000 | bytes 1 | tf_op jit(solution)/shard_map/encode_rows/pallas_call | solution.py:102
  8.9 0.5 collective-permute-start
  9.5 2.6 %collective-permute-start.1 = (bf16[4,128,896]{2,1,0:T(8,128)(2,1)S(1)}, bf16[4,128,896]{2,1,0:T(8,128)(2,1)S(1)}, u32[]{:S(2)}, u32[]{:S(2)}) collective-permute-start(bf16[4,128,896]{2,1,0:T(8,128)(2,1)S(1)} %encode_rows.1.refs_3_), channel_id=1, source_target_pairs={{0,2},{1,3},{2,0},{3,1},{4,6},{5,7},{6,4},{7,5},{8,10},{9,11},{10,... | collective-permute-start | bytes 2752520 | tf_op jit(solution)/shard_map/ppermute | solution.py:445
  12.0 1.5 %collective-permute-start.2 = (bf16[4,128,896]{2,1,0:T(8,128)(2,1)S(1)}, bf16[4,128,896]{2,1,0:T(8,128)(2,1)S(1)}, u32[]{:S(2)}, u32[]{:S(2)}) collective-permute-start(bf16[4,128,896]{2,1,0:T(8,128)(2,1)S(1)} %encode_rows.1.refs_3_), channel_id=1, source_target_pairs={{0,4},{1,5},{2,6},{3,7},{4,0},{5,1},{6,2},{7,3},{8,12},{9,13},{10,... | collective-permute-start | bytes 2752520 | tf_op jit(solution)/shard_map/ppermute | solution.py:445
  13.5 1.6 %collective-permute-start.5 = (bf16[1,448,2048]{2,1,0:T(8,128)(2,1)}, bf16[1,448,2048]{2,1,0:T(8,128)(2,1)}, u32[]{:S(2)}, u32[]{:S(2)}) collective-permute-start(bf16[1,448,2048]{2,1,0:T(8,128)(2,1)} %param.8), channel_id=1, source_target_pairs={{24,0},{0,8},{8,16},{16,24},{25,1},{1,9},{9,17},{17,25},{26,2},{2,... | collective-permute-start | bytes 5505032 | tf_op jit(solution)/shard_map/ppermute | solution.py:440
  15.1 0.0 copy-done.1
  15.1 0.0 copy-done
  15.1 0.1 copy.16
  15.2 0.1 reshape.6.refs_0_
  15.3 0.0 collective-permute-done.refs_4_
  15.3 9.5 %keyvals_rows.2 = (bf16[14,128,4096]{2,1,0:T(8,128)(2,1)}, bf16[896,4096]{1,0:T(8,128)(2,1)S(1)}, f32[8,128]{1,0:T(8,128)S(1)}) custom-call(s32[14]{0:T(128)S(1)} %reshape.6.refs_0_, s32[1]{0:T(128)} %bitcast.refs_1_, bf16[1,896,4096]{2,1,0:T(8,128)(2,1)} %refs_2_.1, bf16[4,128,896]{2,1,0:T(8,128)(2,1)S(1)} %encode_rows.1.refs_3_, ...), custom_call_target="tpu_custom_call" | custom-call | flops 4000000000 | bytes 1 | tf_op jit(solution)/shard_map/keyvals_rows/pallas_call | solution.py:218
  24.8 8.2 %collective-permute-done.1.x_ref = bf16[4,128,896]{2,1,0:T(8,128)(2,1)S(1)} collective-permute-done((bf16[4,128,896]{2,1,0:T(8,128)(2,1)S(1)}, bf16[4,128,896]{2,1,0:T(8,128)(2,1)S(1)}, u32[]{:S(2)}, u32[]{:S(2)}) %collective-permute-start.1) | collective-permute-done | bytes 917536 | tf_op jit(solution)/shard_map/ppermute | solution.py:445
  33.0 1.5 %collective-permute-done.2.y_ref = bf16[4,128,896]{2,1,0:T(8,128)(2,1)S(1)} collective-permute-done((bf16[4,128,896]{2,1,0:T(8,128)(2,1)S(1)}, bf16[4,128,896]{2,1,0:T(8,128)(2,1)S(1)}, u32[]{:S(2)}, u32[]{:S(2)}) %collective-permute-start.2) | collective-permute-done | bytes 917536 | tf_op jit(solution)/shard_map/ppermute | solution.py:445
  34.4 0.6 next_sends.1
  35.0 0.1 collective-permute-start.3
  35.1 0.5 collective-permute-start.4
  35.6 1.5 %collective-permute-start.6 = (bf16[2,128,896]{2,1,0:T(8,128)(2,1)S(1)}, bf16[2,128,896]{2,1,0:T(8,128)(2,1)S(1)}, u32[]{:S(2)}, u32[]{:S(2)}) collective-permute-start(bf16[2,128,896]{2,1,0:T(8,128)(2,1)S(1)} %get-tuple-element.24), channel_id=1, source_target_pairs={{0,4},{1,5},{2,6},{3,7},{4,0},{5,1},{6,2},{7,3},{8,12},{9,13},{10,... | collective-permute-start | bytes 1376264 | tf_op jit(solution)/shard_map/ppermute | solution.py:445
  37.1 0.5 collective-permute-start.7
  37.6 0.0 collective-permute-done.3.refs_4_
  37.6 1.2 %collective-permute-done.4.refs_6_ = bf16[4,128,896]{2,1,0:T(8,128)(2,1)S(1)} collective-permute-done((bf16[4,128,896]{2,1,0:T(8,128)(2,1)S(1)}, bf16[4,128,896]{2,1,0:T(8,128)(2,1)S(1)}, u32[]{:S(2)}, u32[]{:S(2)}) %collective-permute-start.4) | collective-permute-done | bytes 917536 | tf_op jit(solution)/shard_map/ppermute | solution.py:445
  38.9 13.3 %keyvals_rows.3 = (bf16[14,128,4096]{2,1,0:T(8,128)(2,1)}, bf16[896,4096]{1,0:T(8,128)(2,1)S(1)}, f32[8,128]{1,0:T(8,128)S(1)}) custom-call(s32[14]{0:T(128)S(1)} %reshape.6.refs_0_, s32[1]{0:T(128)} %bitcast.refs_1_, bf16[896,4096]{1,0:T(8,128)(2,1)S(1)} %get-tuple-element.17.refs_2_, ...), custom_call_target="tpu_custom_call", output_to_operand_aliasing={{1}: (2, {}), {0}: (7, {})} | custom-call | flops 4000000000 | bytes 1 | tf_op jit(solution)/shard_map/keyvals_rows/pallas_call | solution.py:218
  52.2 0.0 collective-permute-done.6.low_ref
  52.2 0.0 collective-permute-done.7.high_ref
  52.2 0.2 collective-permute-start.8
  52.3 0.4 collective-permute-start.9
  52.8 1.3 %collective-permute-done.8.refs_4_ = bf16[2,128,896]{2,1,0:T(8,128)(2,1)S(1)} collective-permute-done((bf16[2,128,896]{2,1,0:T(8,128)(2,1)S(1)}, bf16[2,128,896]{2,1,0:T(8,128)(2,1)S(1)}, u32[]{:S(2)}, u32[]{:S(2)}) %collective-permute-start.8) | collective-permute-done | bytes 458784 | tf_op jit(solution)/shard_map/ppermute | solution.py:445
  54.1 0.7 collective-permute-done.9.refs_6_
  54.7 6.5 %last_keyvals.1.refs_4_ = bf16[4,128,4096]{2,1,0:T(8,128)(2,1)S(1)} custom-call(s32[14]{0:T(128)S(1)} %reshape.6.refs_0_, s32[1]{0:T(128)} %bitcast.refs_1_, bf16[896,4096]{1,0:T(8,128)(2,1)S(1)} %get-tuple-element.23.refs_2_, bf16[2,128,896]{2,1,0:T(8,128)(2,1)S(1)} %get-tuple-element.27.refs_3_, bf16[2,128,896]{2,1,0:T(8,128)(2,1)S(1)} %collective-permute-done.8.refs_4_, ...), custom_call_target="tpu_custom_call" | custom-call | flops 10000000 | bytes 1 | tf_op jit(solution)/shard_map/last_keyvals/pallas_call | solution.py:286
  61.2 0.0 collective-permute-done.5.refs_3_
  61.2 8.6 %cross_spans.1 = bf16[1,448,2048]{2,1,0:T(8,128)(2,1)} custom-call(s32[14]{0:T(128)S(1)} %reshape.6.refs_0_, s32[1]{0:T(128)} %bitcast.refs_1_, bf16[14,128,4096]{2,1,0:T(8,128)(2,1)} %get-tuple-element.22.refs_2_, bf16[1,448,2048]{2,1,0:T(8,128)(2,1)} %collective-permute-done.5.refs_3_, bf16[4,128,4096]{2,1,0:T(8,128)(2,1)S(1)} %last_keyvals.1.refs_4_), custom_call_target="tpu_custom_call" | custom-call | flops 6000000000 | bytes 1 | tf_op jit(solution)/shard_map/cross_spans/pallas_call | solution.py:370
  (2 shorter events, 0.0 us)
Async XLA Ops:
  0.0 15.1 %copy-start.1 = (s32[1,7,2]{1,2,0:T(2,128)S(1)}, s32[1,7,2]{1,2,0:T(2,128)}, u32[]{:S(2)}) copy-start(s32[1,7,2]{1,2,0:T(2,128)} %param.10) | copy-start | bytes 172
  0.0 15.1 %copy-start = (s32[1,7,2]{1,2,0:T(2,128)S(1)}, s32[1,7,2]{1,2,0:T(2,128)}, u32[]{:S(2)}) copy-start(s32[1,7,2]{1,2,0:T(2,128)} %param.11) | copy-start | bytes 172
  8.9 6.4 %collective-permute-start = (bf16[4,128,896]{2,1,0:T(8,128)(2,1)S(1)}, bf16[4,128,896]{2,1,0:T(8,128)(2,1)}, u32[]{:S(2)}, u32[]{:S(2)}) collective-permute-start(bf16[4,128,896]{2,1,0:T(8,128)(2,1)S(1)} %encode_rows.1.refs_3_), channel_id=1, source_target_pairs={{0,1},{1,0},{2,3},{3,2},{4,5},{5,4},{6,7},{7,6},{8,9},{9,8},{10,11... | collective-permute-start | bytes 2752520 | tf_op jit(solution)/shard_map/ppermute | solution.py:445
  9.5 23.5 %collective-permute-start.1 = (bf16[4,128,896]{2,1,0:T(8,128)(2,1)S(1)}, bf16[4,128,896]{2,1,0:T(8,128)(2,1)S(1)}, u32[]{:S(2)}, u32[]{:S(2)}) collective-permute-start(bf16[4,128,896]{2,1,0:T(8,128)(2,1)S(1)} %encode_rows.1.refs_3_), channel_id=1, source_target_pairs={{0,2},{1,3},{2,0},{3,1},{4,6},{5,7},{6,4},{7,5},{8,10},{9,11},{10,... | collective-permute-start | bytes 2752520 | tf_op jit(solution)/shard_map/ppermute | solution.py:445
  12.0 22.4 %collective-permute-start.2 = (bf16[4,128,896]{2,1,0:T(8,128)(2,1)S(1)}, bf16[4,128,896]{2,1,0:T(8,128)(2,1)S(1)}, u32[]{:S(2)}, u32[]{:S(2)}) collective-permute-start(bf16[4,128,896]{2,1,0:T(8,128)(2,1)S(1)} %encode_rows.1.refs_3_), channel_id=1, source_target_pairs={{0,4},{1,5},{2,6},{3,7},{4,0},{5,1},{6,2},{7,3},{8,12},{9,13},{10,... | collective-permute-start | bytes 2752520 | tf_op jit(solution)/shard_map/ppermute | solution.py:445
  13.5 47.7 %collective-permute-start.5 = (bf16[1,448,2048]{2,1,0:T(8,128)(2,1)}, bf16[1,448,2048]{2,1,0:T(8,128)(2,1)}, u32[]{:S(2)}, u32[]{:S(2)}) collective-permute-start(bf16[1,448,2048]{2,1,0:T(8,128)(2,1)} %param.8), channel_id=1, source_target_pairs={{24,0},{0,8},{8,16},{16,24},{25,1},{1,9},{9,17},{17,25},{26,2},{2,... | collective-permute-start | bytes 5505032 | tf_op jit(solution)/shard_map/ppermute | solution.py:440
  35.0 2.6 %collective-permute-start.3 = (bf16[4,128,896]{2,1,0:T(8,128)(2,1)S(1)}, bf16[4,128,896]{2,1,0:T(8,128)(2,1)S(1)}, u32[]{:S(2)}, u32[]{:S(2)}) collective-permute-start(bf16[4,128,896]{2,1,0:T(8,128)(2,1)S(1)} %get-tuple-element.19.refs_3_), channel_id=1, source_target_pairs={{0,1},{1,0},{2,3},{3,2},{4,5},{5,4},{6,7},{7,6},{8,9},{9,8},{10,11... | collective-permute-start | bytes 2752520 | tf_op jit(solution)/shard_map/ppermute | solution.py:445
  35.1 3.8 %collective-permute-start.4 = (bf16[4,128,896]{2,1,0:T(8,128)(2,1)S(1)}, bf16[4,128,896]{2,1,0:T(8,128)(2,1)S(1)}, u32[]{:S(2)}, u32[]{:S(2)}) collective-permute-start(bf16[4,128,896]{2,1,0:T(8,128)(2,1)S(1)} %get-tuple-element.20.refs_5_), channel_id=1, source_target_pairs={{0,1},{1,0},{2,3},{3,2},{4,5},{5,4},{6,7},{7,6},{8,9},{9,8},{10,11... | collective-permute-start | bytes 2752520 | tf_op jit(solution)/shard_map/ppermute | solution.py:445
  35.6 16.6 %collective-permute-start.6 = (bf16[2,128,896]{2,1,0:T(8,128)(2,1)S(1)}, bf16[2,128,896]{2,1,0:T(8,128)(2,1)S(1)}, u32[]{:S(2)}, u32[]{:S(2)}) collective-permute-start(bf16[2,128,896]{2,1,0:T(8,128)(2,1)S(1)} %get-tuple-element.24), channel_id=1, source_target_pairs={{0,4},{1,5},{2,6},{3,7},{4,0},{5,1},{6,2},{7,3},{8,12},{9,13},{10,... | collective-permute-start | bytes 1376264 | tf_op jit(solution)/shard_map/ppermute | solution.py:445
  37.1 15.1 %collective-permute-start.7 = (bf16[2,128,896]{2,1,0:T(8,128)(2,1)S(1)}, bf16[2,128,896]{2,1,0:T(8,128)(2,1)S(1)}, u32[]{:S(2)}, u32[]{:S(2)}) collective-permute-start(bf16[2,128,896]{2,1,0:T(8,128)(2,1)S(1)} %get-tuple-element.25), channel_id=1, source_target_pairs={{0,2},{1,3},{2,0},{3,1},{4,6},{5,7},{6,4},{7,5},{8,10},{9,11},{10,... | collective-permute-start | bytes 1376264 | tf_op jit(solution)/shard_map/ppermute | solution.py:445
  52.2 1.9 %collective-permute-start.8 = (bf16[2,128,896]{2,1,0:T(8,128)(2,1)S(1)}, bf16[2,128,896]{2,1,0:T(8,128)(2,1)S(1)}, u32[]{:S(2)}, u32[]{:S(2)}) collective-permute-start(bf16[2,128,896]{2,1,0:T(8,128)(2,1)S(1)} %get-tuple-element.27.refs_3_), channel_id=1, source_target_pairs={{0,1},{1,0},{2,3},{3,2},{4,5},{5,4},{6,7},{7,6},{8,9},{9,8},{10,11... | collective-permute-start | bytes 1376264 | tf_op jit(solution)/shard_map/ppermute | solution.py:445
  52.3 2.4 %collective-permute-start.9 = (bf16[2,128,896]{2,1,0:T(8,128)(2,1)S(1)}, bf16[2,128,896]{2,1,0:T(8,128)(2,1)S(1)}, u32[]{:S(2)}, u32[]{:S(2)}) collective-permute-start(bf16[2,128,896]{2,1,0:T(8,128)(2,1)S(1)} %get-tuple-element.28.refs_5_), channel_id=1, source_target_pairs={{0,1},{1,0},{2,3},{3,2},{4,5},{5,4},{6,7},{7,6},{8,9},{9,8},{10,11... | collective-permute-start | bytes 1376264 | tf_op jit(solution)/shard_map/ppermute | solution.py:445
